TPU v7x, 32 devices: a whole 2x2x4 slice. The times are simulated.
32 devices in a mesh: dp: 4 (over z), sx: 4 (over x, core), sy: 2 (over y).
Axes of the slice: x: 2, y: 2, z: 4, core: 2. Of those that a mesh axis runs over, the one named last changes fastest.
Arguments:
- features: bfloat16 [4, 4, 2, 3072, 128], P('dp', 'sx', 'sy'), may hold values from -6 to 6
- cotangent: bfloat16 [4, 4, 2, 3072, 128], P('dp', 'sx', 'sy'), may hold values from -6 to 6
- weights: bfloat16 [27, 128, 128], replicated, may hold values from -0.109375 to 0.109375
- tables: int32 [4, 4, 2, 27, 24], P('dp', 'sx', 'sy'), may hold values from 0 to 56, as said below
- send_lists: int32 [4, 4, 2, 4], P('dp', 'sx', 'sy'), may hold values from 0 to 23, as said below
- counts: int32 [4, 4, 2], P('dp', 'sx', 'sy'), may hold values from 6 to 24, as said below
Outputs:
- output: bfloat16 [4, 4, 2, 3072, 128], P('dp', 'sx', 'sy')
- input_grad: bfloat16 [4, 4, 2, 3072, 128], P('dp', 'sx', 'sy')
- weight_grad: float32 [27, 128, 128], replicated
Inputs may be any that keep to these rules, and one draw needn't show every extreme that they name: `tables`: entries below 24 name a block of the tile, 24 + n * 4 + s' the s'-th sent block of neighbour direction n, 56 the empty block; under offset 27 // 2 every block reads itself. `send_lists`: the 4 blocks of one tile are distinct. `counts`: some tile has all 24 blocks active.
All inputs are finite; a program needn't handle non-finite values.
Results may differ from a plain program's by a relative error of at most 0.001.
Values may be sent and summed in bfloat16 or wider, within the bound.
No kernel may reach another device: no remote copies, remote signals or barrier semaphores. Data moves between devices by JAX's collectives and lax.ppermute only.
A program may use at most 64 MiB of HBM per device.

v0:
```python
import math

import jax
import jax.numpy as jnp
from jax import lax
from jax.sharding import PartitionSpec as P

directions = ((-1, -1), (-1, 0), (-1, 1), (0, -1), (0, 1), (1, -1), (1, 0), (1, 1))


def shifted(block, axis, distance):
    devices = range(lax.axis_size(axis))
    route = [(i - distance, i) for i in devices if i - distance in devices]
    return lax.ppermute(block, axis, route)


def padded(cells, sides, width):
    for axis, dim in sides:
        count = lax.axis_size(axis)
        ends = count - 1
        head = lax.slice_in_dim(cells, 0, width, axis=dim)
        tail = lax.slice_in_dim(cells, cells.shape[dim] - width, cells.shape[dim], axis=dim)
        cells = jnp.concatenate(
            [
                lax.ppermute(tail, axis, [(i, (i + 1) % count) for i in range(ends)]),
                cells,
                lax.ppermute(head, axis, [((i + 1) % count, i) for i in range(ends)]),
            ],
            axis=dim,
        )
    return cells


def local(features, cotangent, weights, tables, send_lists, counts):
    num_blocks = tables.shape[4]
    num_sent = send_lists.shape[3]
    offsets = weights.shape[0]
    channels = weights.shape[1]
    width_block = features.shape[3] // num_blocks
    group_size = 4
    active = (jnp.arange(num_blocks) < counts.reshape(())).astype(jnp.bfloat16)[:, None, None]
    active_full = active.astype(jnp.float32)
    blocks_in = features.reshape(num_blocks, width_block, channels) * active
    blocks_grad = cotangent.reshape(num_blocks, width_block, channels) * active
    offset_table = tables.reshape(offsets, num_blocks)
    sent_ids = send_lists.reshape(num_sent)
    groups = jnp.arange(num_blocks // group_size)

    def grad_group(accum, group):
        start = group * group_size
        picks = lax.dynamic_slice_in_dim(offset_table, start, group_size, 1)
        grad_rows = lax.dynamic_slice_in_dim(blocks_grad, start, group_size, 0)
        contrib = jnp.einsum(
            "gvd,kcd->kgvc", grad_rows, weights, preferred_element_type=jnp.float32
        )
        accum = accum.at[picks.reshape(-1)].add(
            contrib.reshape(offsets * group_size, width_block, channels)
        )
        return (accum, None)

    num_ext = num_blocks + 8 * num_sent + 1
    grad_ext, unused_rows = lax.scan(
        grad_group, jnp.zeros((num_ext, width_block, channels), jnp.float32), groups
    )
    halo_grads = grad_ext[num_blocks : num_blocks + 8 * num_sent].reshape(
        8, num_sent * width_block, channels
    )
    received = jnp.zeros((num_sent * width_block, channels), jnp.float32)
    for slot_index, (step_x, step_y) in enumerate(directions):
        portion = halo_grads[slot_index]
        if step_x != 0:
            portion = shifted(portion, "sx", step_x)
        if step_y != 0:
            portion = shifted(portion, "sy", step_y)
        received = received + portion
    local_grad = (
        grad_ext[:num_blocks].at[sent_ids].add(received.reshape(num_sent, width_block, channels))
    )
    input_grad = (local_grad * active_full).astype(jnp.bfloat16).reshape(features.shape)
    outgoing = blocks_in[sent_ids].reshape(1, 1, num_sent * width_block, channels)
    bordered = padded(outgoing, (("sx", 0), ("sy", 1)), 1)
    neighbours = [
        bordered[1 + step_x, 1 + step_y].reshape(num_sent, width_block, channels)
        for step_x, step_y in directions
    ]
    extended = jnp.concatenate(
        [blocks_in] + neighbours + [jnp.zeros((1, width_block, channels), jnp.bfloat16)], axis=0
    )

    def forward_group(accum, group):
        start = group * group_size
        picks = lax.dynamic_slice_in_dim(offset_table, start, group_size, 1)
        gathered = extended[picks]
        grad_rows = lax.dynamic_slice_in_dim(blocks_grad, start, group_size, 0)
        rows_active = lax.dynamic_slice_in_dim(active_full, start, group_size, 0)
        outputs = jnp.einsum("kgvc,kcd->gvd", gathered, weights, preferred_element_type=jnp.float32)
        accum = accum + jnp.einsum(
            "kgvc,gvd->kcd", gathered, grad_rows, preferred_element_type=jnp.float32
        )
        return (accum, (outputs * rows_active).astype(jnp.bfloat16))

    weight_part, outputs = lax.scan(
        forward_group, jnp.zeros((offsets, channels, channels), jnp.float32), groups
    )
    output = outputs.reshape(features.shape)
    total = (
        num_blocks * width_block * lax.axis_size("dp") * lax.axis_size("sx") * lax.axis_size("sy")
    )
    scaled_part = weight_part * (1.0 / math.sqrt(total))
    weight_grad = lax.psum(scaled_part, ("dp", "sx", "sy"))
    return (output, input_grad, weight_grad)


def solution(mesh):
    return jax.shard_map(
        local,
        mesh=mesh,
        in_specs=(
            P("dp", "sx", "sy", None, None),
            P("dp", "sx", "sy", None, None),
            P(),
            P("dp", "sx", "sy", None, None),
            P("dp", "sx", "sy", None),
            P("dp", "sx", "sy"),
        ),
        out_specs=(P("dp", "sx", "sy", None, None), P("dp", "sx", "sy", None, None), P()),
        check_vma=False,
    )
```

profile of v0, /device:TPU:0, one launch (start us, length us, event | category | flops | bytes accessed | tf_op | source)
XLA Modules:
  0.0 473.3 jit_solution(15077113721366532922)
XLA Ops:
  8.5 3.2 constant_dynamic-update-slice_fusion.9
  19.8 184.8 %while.23 = (s32[]{:T(128)}, f32[57,128,128]{2,1,0:T(8,128)}, s32[6]{0:T(128)S(1)}, s32[27,24]{1,0:T(8,128)}, bf16[24,128,128]{2,1,0:T(8,128)(2,1)}, /*index=5*/...) while((s32[]{:T(128)}, f32[57,128,128]{2,1,0:T(8,128)}, s32[6]{0:T(128)S(1)}, ...), condition=%wide.region_4.5_spmd, body=%wide.region_2.0_spmd.sunk | while | flops 454754624 | bytes 43486336 | solution.py:62
  24.3 3.3 copy.22
  27.6 22.9 %scatter_fusion = f32[57,128,128]{2,1,0:T(8,128)} fusion(f32[57,128,128]{2,1,0:T(8,128)} %get-tuple-element.307, s32[108]{0:T(128)S(1)} %fusion.33, f32[108,128,128]{2,1,0:T(8,128)} %bitcast.107), kind=kCustom, calls=%fused_computation.2.clone.1 | custom fusion | flops 1769472 | bytes 21234096 | tf_op jit(solution)/shard_map/while/body/eval_jaxpr/scatter-add | solution.py:56
  55.0 3.3 copy.22
  58.3 22.9 %scatter_fusion = f32[57,128,128]{2,1,0:T(8,128)} fusion(f32[57,128,128]{2,1,0:T(8,128)} %get-tuple-element.307, s32[108]{0:T(128)S(1)} %fusion.33, f32[108,128,128]{2,1,0:T(8,128)} %bitcast.107), kind=kCustom, calls=%fused_computation.2.clone.1 | custom fusion | flops 1769472 | bytes 21234096 | tf_op jit(solution)/shard_map/while/body/eval_jaxpr/scatter-add | solution.py:56
  85.7 3.3 copy.22
  89.1 23.0 %scatter_fusion = f32[57,128,128]{2,1,0:T(8,128)} fusion(f32[57,128,128]{2,1,0:T(8,128)} %get-tuple-element.307, s32[108]{0:T(128)S(1)} %fusion.33, f32[108,128,128]{2,1,0:T(8,128)} %bitcast.107), kind=kCustom, calls=%fused_computation.2.clone.1 | custom fusion | flops 1769472 | bytes 21234096 | tf_op jit(solution)/shard_map/while/body/eval_jaxpr/scatter-add | solution.py:56
  116.6 3.3 copy.22
  119.9 22.9 %scatter_fusion = f32[57,128,128]{2,1,0:T(8,128)} fusion(f32[57,128,128]{2,1,0:T(8,128)} %get-tuple-element.307, s32[108]{0:T(128)S(1)} %fusion.33, f32[108,128,128]{2,1,0:T(8,128)} %bitcast.107), kind=kCustom, calls=%fused_computation.2.clone.1 | custom fusion | flops 1769472 | bytes 21234096 | tf_op jit(solution)/shard_map/while/body/eval_jaxpr/scatter-add | solution.py:56
  147.4 3.3 copy.22
  150.7 23.0 %scatter_fusion = f32[57,128,128]{2,1,0:T(8,128)} fusion(f32[57,128,128]{2,1,0:T(8,128)} %get-tuple-element.307, s32[108]{0:T(128)S(1)} %fusion.33, f32[108,128,128]{2,1,0:T(8,128)} %bitcast.107), kind=kCustom, calls=%fused_computation.2.clone.1 | custom fusion | flops 1769472 | bytes 21234096 | tf_op jit(solution)/shard_map/while/body/eval_jaxpr/scatter-add | solution.py:56
  178.2 3.3 copy.22
  181.5 23.1 %scatter_fusion = f32[57,128,128]{2,1,0:T(8,128)} fusion(f32[57,128,128]{2,1,0:T(8,128)} %get-tuple-element.307, s32[108]{0:T(128)S(1)} %fusion.33, f32[108,128,128]{2,1,0:T(8,128)} %bitcast.107), kind=kCustom, calls=%fused_computation.2.clone.1 | custom fusion | flops 1769472 | bytes 21234096 | tf_op jit(solution)/shard_map/while/body/eval_jaxpr/scatter-add | solution.py:56
  204.7 4.2 collective-permute-start.2
  211.8 3.6 collective-permute-start.14
  216.7 3.8 collective-permute-start.13
  226.1 9.6 %collective-permute-done.3 = bf16[3,1,512,128]{3,2,1,0:T(8,128)(2,1)S(1)} collective-permute-done((bf16[3,1,512,128]{3,2,1,0:T(8,128)(2,1)S(1)}, bf16[3,1,512,128]{3,2,1,0:T(8,128)(2,1)S(1)}, u32[]{:S(2)}, u32[]{:S(2)}) %collective-permute-start.3) | collective-permute-done | bytes 393248 | tf_op jit(solution)/shard_map/ppermute | solution.py:27
  243.0 79.9 %while.24 = (s32[]{:T(128)}, f32[27,128,128]{2,1,0:T(8,128)}, bf16[6,4,128,128]{3,2,1,0:T(8,128)(2,1)}, s32[6]{0:T(128)}, s32[27,24]{1,0:T(8,128)}, /*index=5*/b...) while((s32[]{:T(128)}, f32[27,128,128]{2,1,0:T(8,128)}, ...), condition=%wide.region_1.0_spmd.clone, body=%wide.region_0.1_spmd.clone.sunk | while | flops 906986816 | bytes 33004880 | solution.py:102
  329.8 4.6 collective-permute-start.15
  335.7 4.6 collective-permute-start.8
  343.3 3.9 collective-permute-done.12
  349.9 4.1 collective-permute-done.5
  357.1 106.4 %all-reduce.2.cloned.1.call-done = f32[27,128,128]{2,1,0:T(8,128)} async-done(((f32[27,128,128]{2,1,0:T(8,128)}), f32[27,128,128]{2,1,0:T(8,128)}) %all-reduce.2.cloned.1.call-update) | async-done | bytes 1769488 | tf_op jit(solution)/shard_map/psum | solution.py:110
  (162 shorter events, 144.4 us)
Async XLA Ops:
  7.2 456.4 %all-reduce.2.cloned.1.call-start = ((), (), s32[]{:S(2)}) async-start(), calls=%async_computation | async-start | bytes 3538944 | tf_op jit(solution)/shard_map/psum | solution.py:110
  8.5 8.2 %copy-start.3 = (s32[1,1,1,27,24]{3,4,2,1,0:T(8,128)S(1)}, s32[1,1,1,27,24]{3,4,2,1,0:T(8,128)}, u32[]{:S(2)}) copy-start(s32[1,1,1,27,24]{3,4,2,1,0:T(8,128)} %param.13) | copy-start | bytes 7780
  12.3 192.3 %collective-permute-start.1 = (bf16[1,1,512,128]{3,2,1,0:T(8,128)(2,1)S(1)}, bf16[1,1,512,128]{3,2,1,0:T(8,128)(2,1)S(1)}, u32[]{:S(2)}, u32[]{:S(2)}) collective-permute-start(bf16[1,1,512,128]{3,2,1,0:T(8,128)(2,1)S(1)} %bitcast.116), channel_id=1, source_target_pairs={{2,0},{4,2},{6,4},{3,1},{5,3},{7,5},{10,8},{12,10},{14,12},{11,9},... | collective-permute-start | bytes 393224 | tf_op jit(solution)/shard_map/ppermute | solution.py:27
  13.6 191.0 %collective-permute-start = (bf16[1,1,512,128]{3,2,1,0:T(8,128)(2,1)S(1)}, bf16[1,1,512,128]{3,2,1,0:T(8,128)(2,1)S(1)}, u32[]{:S(2)}, u32[]{:S(2)}) collective-permute-start(bf16[1,1,512,128]{3,2,1,0:T(8,128)(2,1)S(1)} %bitcast.117), channel_id=1, source_target_pairs={{0,2},{2,4},{4,6},{1,3},{3,5},{5,7},{8,10},{10,12},{12,14},{9,11},... | collective-permute-start | bytes 393224 | tf_op jit(solution)/shard_map/ppermute | solution.py:25
  204.7 18.8 %collective-permute-start.2 = (bf16[3,1,512,128]{3,2,1,0:T(8,128)(2,1)S(1)}, bf16[3,1,512,128]{3,2,1,0:T(8,128)(2,1)S(1)}, u32[]{:S(2)}, u32[]{:S(2)}) collective-permute-start(bf16[3,1,512,128]{3,2,1,0:T(8,128)(2,1)S(1)} %pad_maximum_fusion), channel_id=1, source_target_pairs={{0,1},{2,3},{4,5},{6,7},{8,9},{10,11},{12,13},{14,15},{16,17},{18,... | collective-permute-start | bytes 1179656 | tf_op jit(solution)/shard_map/ppermute | solution.py:25
  211.8 111.1 %collective-permute-start.14 = (f32[512,128]{1,0:T(8,128)}, f32[512,128]{1,0:T(8,128)}, u32[]{:S(2)}, u32[]{:S(2)}) collective-permute-start(f32[512,128]{1,0:T(8,128)} %bitcast.30), channel_id=1, source_target_pairs={{0,2},{2,4},{4,6},{1,3},{3,5},{5,7},{8,10},{10,12},{12,14},{9,11},... | collective-permute-start | bytes 786440 | tf_op jit(solution)/shard_map/ppermute | solution.py:14
  215.4 108.8 %collective-permute-start.6 = (f32[512,128]{1,0:T(8,128)}, f32[512,128]{1,0:T(8,128)}, u32[]{:S(2)}, u32[]{:S(2)}) collective-permute-start(f32[512,128]{1,0:T(8,128)} %bitcast.24), channel_id=1, source_target_pairs={{2,0},{4,2},{6,4},{3,1},{5,3},{7,5},{10,8},{12,10},{14,12},{11,9},... | collective-permute-start | bytes 786440 | tf_op jit(solution)/shard_map/ppermute | solution.py:14
  216.7 111.8 %collective-permute-start.13 = (f32[512,128]{1,0:T(8,128)}, f32[512,128]{1,0:T(8,128)}, u32[]{:S(2)}, u32[]{:S(2)}) collective-permute-start(f32[512,128]{1,0:T(8,128)} %bitcast.29), channel_id=1, source_target_pairs={{0,2},{2,4},{4,6},{1,3},{3,5},{5,7},{8,10},{10,12},{12,14},{9,11},... | collective-permute-start | bytes 786440 | tf_op jit(solution)/shard_map/ppermute | solution.py:14
  220.5 109.3 %collective-permute-start.11 = (f32[512,128]{1,0:T(8,128)}, f32[512,128]{1,0:T(8,128)}, u32[]{:S(2)}, u32[]{:S(2)}) collective-permute-start(f32[512,128]{1,0:T(8,128)} %bitcast.28), channel_id=1, source_target_pairs={{0,2},{2,4},{4,6},{1,3},{3,5},{5,7},{8,10},{10,12},{12,14},{9,11},... | collective-permute-start | bytes 786440 | tf_op jit(solution)/shard_map/ppermute | solution.py:14
  223.5 12.3 %collective-permute-start.3 = (bf16[3,1,512,128]{3,2,1,0:T(8,128)(2,1)S(1)}, bf16[3,1,512,128]{3,2,1,0:T(8,128)(2,1)S(1)}, u32[]{:S(2)}, u32[]{:S(2)}) collective-permute-start(bf16[3,1,512,128]{3,2,1,0:T(8,128)(2,1)S(1)} %pad_maximum_fusion), channel_id=1, source_target_pairs={{1,0},{3,2},{5,4},{7,6},{9,8},{11,10},{13,12},{15,14},{17,16},{19,... | collective-permute-start | bytes 1179656 | tf_op jit(solution)/shard_map/ppermute | solution.py:27
  235.7 98.7 %collective-permute-start.10 = (f32[512,128]{1,0:T(8,128)}, f32[512,128]{1,0:T(8,128)}, u32[]{:S(2)}, u32[]{:S(2)}) collective-permute-start(f32[512,128]{1,0:T(8,128)} %bitcast.27), channel_id=1, source_target_pairs={{0,1},{2,3},{4,5},{6,7},{8,9},{10,11},{12,13},{14,15},{16,17},{18,... | collective-permute-start | bytes 786440 | tf_op jit(solution)/shard_map/ppermute | solution.py:14
  249.2 3.1 copy-start
  262.5 3.1 copy-start
  275.8 3.1 copy-start
  289.1 3.1 copy-start
  302.4 3.1 copy-start
  315.7 3.1 copy-start
  322.9 12.8 %collective-permute-start.7 = (f32[512,128]{1,0:T(8,128)}, f32[512,128]{1,0:T(8,128)S(1)}, u32[]{:S(2)}, u32[]{:S(2)}) collective-permute-start(f32[512,128]{1,0:T(8,128)} %bitcast.127), channel_id=1, source_target_pairs={{2,0},{4,2},{6,4},{3,1},{5,3},{7,5},{10,8},{12,10},{14,12},{11,9},... | collective-permute-start | bytes 786440 | tf_op jit(solution)/shard_map/ppermute | solution.py:14
  324.2 16.1 %collective-permute-start.4 = (f32[512,128]{1,0:T(8,128)}, f32[512,128]{1,0:T(8,128)S(1)}, u32[]{:S(2)}, u32[]{:S(2)}) collective-permute-start(f32[512,128]{1,0:T(8,128)} %bitcast.126), channel_id=1, source_target_pairs={{2,0},{4,2},{6,4},{3,1},{5,3},{7,5},{10,8},{12,10},{14,12},{11,9},... | collective-permute-start | bytes 786440 | tf_op jit(solution)/shard_map/ppermute | solution.py:14
  328.5 14.6 %collective-permute-start.9 = (f32[512,128]{1,0:T(8,128)S(1)}, f32[512,128]{1,0:T(8,128)S(1)}, u32[]{:S(2)}, u32[]{:S(2)}) collective-permute-start(f32[512,128]{1,0:T(8,128)S(1)} %bitcast.125), channel_id=1, source_target_pairs={{1,0},{3,2},{5,4},{7,6},{9,8},{11,10},{13,12},{15,14},{17,16},{19,... | collective-permute-start | bytes 786440 | tf_op jit(solution)/shard_map/ppermute | solution.py:14
  329.8 13.5 %collective-permute-start.15 = (f32[512,128]{1,0:T(8,128)}, f32[512,128]{1,0:T(8,128)S(1)}, u32[]{:S(2)}, u32[]{:S(2)}) collective-permute-start(f32[512,128]{1,0:T(8,128)} %collective-permute-done.14), channel_id=1, source_target_pairs={{0,1},{2,3},{4,5},{6,7},{8,9},{10,11},{12,13},{14,15},{16,17},{18,... | collective-permute-start | bytes 786440 | tf_op jit(solution)/shard_map/ppermute | solution.py:14
  334.4 12.8 %collective-permute-start.12 = (f32[512,128]{1,0:T(8,128)}, f32[512,128]{1,0:T(8,128)S(1)}, u32[]{:S(2)}, u32[]{:S(2)}) collective-permute-start(f32[512,128]{1,0:T(8,128)} %collective-permute-done.11), channel_id=1, source_target_pairs={{1,0},{3,2},{5,4},{7,6},{9,8},{11,10},{13,12},{15,14},{17,16},{19,... | collective-permute-start | bytes 786440 | tf_op jit(solution)/shard_map/ppermute | solution.py:14
  335.7 14.2 %collective-permute-start.8 = (f32[512,128]{1,0:T(8,128)S(1)}, f32[512,128]{1,0:T(8,128)S(1)}, u32[]{:S(2)}, u32[]{:S(2)}) collective-permute-start(f32[512,128]{1,0:T(8,128)S(1)} %collective-permute-done.7), channel_id=1, source_target_pairs={{0,1},{2,3},{4,5},{6,7},{8,9},{10,11},{12,13},{14,15},{16,17},{18,... | collective-permute-start | bytes 786440 | tf_op jit(solution)/shard_map/ppermute | solution.py:14
  340.3 13.7 %collective-permute-start.5 = (f32[512,128]{1,0:T(8,128)S(1)}, f32[512,128]{1,0:T(8,128)S(1)}, u32[]{:S(2)}, u32[]{:S(2)}) collective-permute-start(f32[512,128]{1,0:T(8,128)S(1)} %collective-permute-done.4), channel_id=1, source_target_pairs={{1,0},{3,2},{5,4},{7,6},{9,8},{11,10},{13,12},{15,14},{17,16},{19,... | collective-permute-start | bytes 786440 | tf_op jit(solution)/shard_map/ppermute | solution.py:14
  (7 other events, 10.3 us)
Sparse Core Ops, SparseCore 0:
  328.6 134.8 all-reduce.1
where the time goes:
time: 477 us; the launch traced here: 473 us
  other arithmetic  153 us (32%)
  waiting for transfers between devices  127 us (27%)
  local copies, waits for them, and re-layouts  81.9 us (17%)
  matrix products  49.6 us (10%)
  starting transfers between devices  39.3 us (8%)
  between operations  14.9 us (3%)
  loops' own time  7.98 us (2%)
    scatter-add x6, other arithmetic, grad_group(): accum.at[picks.reshape(-1)]  138 us
    psum x1, waiting for transfers between devices, local(): weight_grad = lax.psum(scaled_part, ('dp', 'sx', 'sy'))  106 us
    ppermute x12, starting transfers between devices, shifted(): return lax.ppermute(block, axis, route)  29.4 us
    transpose x6, local copies, waits for them, and re-layouts, grad_group(): jnp.einsum('gvd,kcd->kgvc', grad_rows, weights, preferred_element_type=jn...  20.1 us
    dot_general x6, matrix products, forward_group(): jnp.einsum('kgvc,kcd->gvd', gathered, weights, preferred_element_type=jnp...  18.2 us
    dot_general x6, matrix products, forward_group(): jnp.einsum('kgvc,gvd->kcd', gathered, grad_rows, preferred_element_type=j...  17.3 us
    gather x6, local copies, waits for them, and re-layouts, forward_group(): gathered = extended[picks]  16.4 us
    dot_general x6, matrix products, grad_group(): jnp.einsum('gvd,kcd->kgvc', grad_rows, weights, preferred_element_type=jn...  14 us
  transfers between devices with their start and end apart: 17, of which 6 were waited for; matrix products, arithmetic and copies ran while one was open for 57% of the time, Pallas kernels for 0%

commit v1 on v0

v1 whole, which is shorter than its diff:
```python
import functools
import math

import jax
import jax.numpy as jnp
from jax import lax
from jax.experimental import pallas as pl
from jax.experimental.pallas import tpu as pltpu
from jax.sharding import PartitionSpec as P

AXES = ("dp", "sx", "sy")
F32 = jnp.float32
BF16 = jnp.bfloat16
VMEM = pl.BlockSpec(memory_space=pltpu.VMEM)
SMEM = pl.BlockSpec(memory_space=pltpu.SMEM)
HBM = pl.BlockSpec(memory_space=pl.ANY)


def params():
    return pltpu.CompilerParams(vmem_limit_bytes=24 * 2**20)


def cost(flops):
    return pl.CostEstimate(flops=flops, bytes_accessed=4 * 2**20, transcendentals=0)


def outgoing_kernel(sent_ref, count_ref, x_ref, out_ref, sems):
    num_sent = out_ref.shape[0]
    copies = [
        pltpu.make_async_copy(x_ref.at[sent_ref[s]], out_ref.at[s], sems.at[s])
        for s in range(num_sent)
    ]
    for copy in copies:
        copy.start()
    for copy in copies:
        copy.wait()
    for s in range(num_sent):

        @pl.when(sent_ref[s] >= count_ref[0])
        def _():
            out_ref[s] = jnp.zeros(out_ref.shape[1:], out_ref.dtype)


def outgoing(sent_ids, count, blocks):
    num_sent = sent_ids.shape[0]
    return pl.pallas_call(
        outgoing_kernel,
        out_shape=jax.ShapeDtypeStruct((num_sent,) + blocks.shape[1:], blocks.dtype),
        in_specs=[SMEM, SMEM, HBM],
        out_specs=VMEM,
        scratch_shapes=[pltpu.SemaphoreType.DMA((num_sent,))],
        compiler_params=params(),
    )(sent_ids, count, blocks)


def input_terms_kernel(picks, grad_ref, weight_ref, own_ref, *rest):
    *halo_refs, accum = rest
    num_blocks, rows, channels = grad_ref.shape
    offsets = weight_ref.shape[0] // channels
    accum[...] = jnp.zeros_like(accum)

    def term(o, matrix):
        return lax.dot_general(
            grad_ref[o], matrix, (((1,), (1,)), ((), ())), preferred_element_type=F32
        )

    def two_offsets(pair, carry):
        start = pl.multiple_of(pair * 2 * channels, 2 * channels)
        matrix = weight_ref[pl.ds(start, 2 * channels), :]
        for o in range(num_blocks):
            both = term(o, matrix)
            accum[picks[2 * pair * num_blocks + o]] += both[:, :channels]
            accum[picks[(2 * pair + 1) * num_blocks + o]] += both[:, channels:]
        return carry

    lax.fori_loop(0, offsets // 2, two_offsets, 0)
    if offsets % 2:
        matrix = weight_ref[(offsets - 1) * channels :, :]
        for o in range(num_blocks):
            accum[picks[(offsets - 1) * num_blocks + o]] += term(o, matrix)
    own_ref[...] = accum[:num_blocks]
    start = num_blocks
    for ref in halo_refs:
        ref[...] = accum[start : start + ref.shape[0]]
        start += ref.shape[0]


def input_terms(picks, grad, weights, halo_sizes):
    num_blocks, rows, channels = grad.shape
    sizes = (num_blocks,) + tuple(halo_sizes)
    return pl.pallas_call(
        input_terms_kernel,
        out_shape=[jax.ShapeDtypeStruct((n, rows, channels), F32) for n in sizes],
        in_specs=[SMEM, VMEM, VMEM],
        out_specs=[VMEM] * len(sizes),
        scratch_shapes=[pltpu.VMEM((sum(sizes) + 1, rows, channels), F32)],
        compiler_params=params(),
        cost_estimate=cost(10 * 10**9),
    )(picks, grad, weights.reshape(-1, channels))


def weight_terms_kernel(scale, chunks, me_ref, picks, grad_ref, *rest):
    *block_refs, keep_ref, send_ref, turned, accum = rest
    channels = grad_ref.shape[1]
    rows = block_refs[0].shape[1]
    num_blocks = grad_ref.shape[0] // rows
    offsets = accum.shape[0] // channels
    start = 0
    for ref in block_refs:
        for e in range(ref.shape[0]):
            turned[start + e] = ref[e].T
        start += ref.shape[0]
    turned[start] = jnp.zeros(turned.shape[1:], turned.dtype)
    accum[...] = jnp.zeros_like(accum)

    def two_blocks(pair, carry):
        first = pl.multiple_of(pair * 2 * rows, 2 * rows)
        grads = grad_ref[pl.ds(first, 2 * rows), :]
        for k in range(offsets):
            left = turned[picks[k * num_blocks + 2 * pair]]
            right = turned[picks[k * num_blocks + 2 * pair + 1]]
            accum[k * channels : (k + 1) * channels, :] += jnp.dot(
                jnp.concatenate([left, right], axis=1), grads, preferred_element_type=F32
            )
        return carry

    lax.fori_loop(0, num_blocks // 2, two_blocks, 0)
    size = accum.shape[0] // chunks
    for r in range(chunks):
        ref, place = (keep_ref, r) if r < chunks // 2 else (send_ref, r - chunks // 2)
        first = pl.multiple_of((me_ref[0] ^ r) * size, size)
        ref[place] = accum[pl.ds(first, size), :] * scale


def weight_terms(me, picks, grad, blocks, offsets, scale, chunks):
    num_blocks, rows, channels = grad.shape
    total = sum(b.shape[0] for b in blocks) + 1
    half = jax.ShapeDtypeStruct((chunks // 2, offsets * channels // chunks, channels), F32)
    return pl.pallas_call(
        functools.partial(weight_terms_kernel, scale, chunks),
        out_shape=[half, half],
        in_specs=[SMEM, SMEM, VMEM] + [VMEM] * len(blocks),
        out_specs=[VMEM, VMEM],
        scratch_shapes=[
            pltpu.VMEM((total, channels, rows), BF16),
            pltpu.VMEM((offsets * channels, channels), F32),
        ],
        compiler_params=params(),
        cost_estimate=cost(10 * 10**9),
    )(me, picks, grad.reshape(-1, channels), *blocks)


def output_kernel(group, picks, weight_ref, *rest):
    *block_refs, out_ref, held = rest
    total, rows, channels = held.shape
    offsets = weight_ref.shape[0] // channels
    num_blocks = out_ref.shape[0] // rows
    start = 0
    for ref in block_refs:
        held[start : start + ref.shape[0]] = ref[...]
        start += ref.shape[0]
    held[start] = jnp.zeros(held.shape[1:], held.dtype)

    def some_blocks(index, carry):
        accum = jnp.zeros((group * rows, channels), F32)
        for k in range(0, offsets, 2):
            pair = range(k, min(k + 2, offsets))
            gathered = [
                jnp.concatenate(
                    [held[picks[kk * num_blocks + index * group + j]] for kk in pair], axis=1
                )
                for j in range(group)
            ]
            accum += jnp.dot(
                jnp.concatenate(gathered, axis=0),
                weight_ref[k * channels : (k + len(pair)) * channels, :],
                preferred_element_type=F32,
            )
        first = pl.multiple_of(index * group * rows, group * rows)
        out_ref[pl.ds(first, group * rows), :] = accum.astype(BF16)
        return carry

    lax.fori_loop(0, num_blocks // group, some_blocks, 0)


def output_blocks(picks, weights, blocks):
    num_blocks, rows, channels = blocks[0].shape
    total = sum(b.shape[0] for b in blocks) + 1
    return pl.pallas_call(
        functools.partial(output_kernel, 4),
        out_shape=jax.ShapeDtypeStruct((num_blocks * rows, channels), BF16),
        in_specs=[SMEM, VMEM] + [VMEM] * len(blocks),
        out_specs=VMEM,
        scratch_shapes=[pltpu.VMEM((total, rows, channels), BF16)],
        compiler_params=params(),
        cost_estimate=cost(10 * 10**9),
    )(picks, weights.reshape(-1, channels), *blocks)


def input_grad_kernel(sent_ref, count_ref, own_ref, *rest):
    *returned_refs, out_ref = rest
    num_blocks = own_ref.shape[0]
    for b in range(num_blocks):
        keep = jnp.where(b < count_ref[0], 1.0, 0.0)
        out_ref[b] = (own_ref[b] * keep).astype(BF16)
    for s in range(returned_refs[0].shape[0]):
        b = sent_ref[s]
        keep = jnp.where(b < count_ref[0], 1.0, 0.0)
        returned = returned_refs[0][s]
        for ref in returned_refs[1:]:
            returned = returned + ref[s]
        out_ref[b] = ((own_ref[b] + returned) * keep).astype(BF16)


def input_grad_blocks(sent_ids, count, own, returned):
    return pl.pallas_call(
        input_grad_kernel,
        out_shape=jax.ShapeDtypeStruct(own.shape, BF16),
        in_specs=[SMEM, SMEM, VMEM] + [VMEM] * len(returned),
        out_specs=VMEM,
        compiler_params=params(),
        cost_estimate=cost(10**9),
    )(sent_ids, count, own, *returned)


def assemble_kernel(me_ref, near_ref, far_ref, out_ref, sems):
    half = near_ref.shape[0]
    copies = []
    for r in range(2 * half):
        source = near_ref.at[r] if r < half else far_ref.at[r - half]
        copies.append(pltpu.make_async_copy(source, out_ref.at[me_ref[0] ^ r], sems.at[r]))
    for copy in copies:
        copy.start()
    for copy in copies:
        copy.wait()


def assemble(me, near, far):
    half, size, channels = near.shape
    return pl.pallas_call(
        assemble_kernel,
        out_shape=jax.ShapeDtypeStruct((2 * half, size, channels), F32),
        in_specs=[SMEM, HBM, HBM],
        out_specs=HBM,
        scratch_shapes=[pltpu.SemaphoreType.DMA((2 * half,))],
        compiler_params=params(),
    )(me, near, far)


def local(features, cotangent, weights, tables, send_lists, counts):
    num_blocks = tables.shape[4]
    num_sent = send_lists.shape[3]
    offsets, channels = weights.shape[0], weights.shape[1]
    width = features.shape[3] // num_blocks
    size_z, size_x, size_y = (lax.axis_size(a) for a in AXES)
    scene, tile_x, tile_y = (lax.axis_index(a) for a in AXES)
    blocks = features.reshape(num_blocks, width, channels)
    grads = cotangent.reshape(num_blocks, width, channels)
    sent_ids = send_lists.reshape(num_sent)
    count = counts.reshape(1)

    odd = tile_x % 2
    inner = [(i, i ^ 1) for i in range(size_x) if (i ^ 1) < size_x]
    outer = [(i, i + 1) for i in range(1, size_x - 1, 2)]
    outer = outer + [(j, i) for i, j in outer]
    if size_y == 2:
        along_y = [[(0, 1), (1, 0)]]
    else:
        along_y = [
            [(i, i + 1) for i in range(size_y - 1)],
            [(i + 1, i) for i in range(size_y - 1)],
        ]
    sides = len(along_y)
    per_x = (1 + sides) * num_sent

    def to_blocks(array):
        return array.reshape(-1, width, channels)

    def to_rows(array):
        return array.reshape(-1, channels)

    table = tables.reshape(offsets, num_blocks)
    code = table - num_blocks
    number = code // num_sent
    cell = number + (number >= 4)
    step_x, step_y = cell // 3 - 1, cell % 3 - 1
    slot = code % num_sent
    near_x, near_y = tile_x + step_x, tile_y + step_y
    inside = (near_x >= 0) & (near_x < size_x) & (near_y >= 0) & (near_y < size_y)
    if size_y == 2:
        side = (step_y != 0).astype(jnp.int32)
    else:
        side = jnp.where(step_y == 0, 0, jnp.where(step_y < 0, 1, 2))
    toward = 1 - 2 * odd
    beyond_x = jnp.where(step_x == toward, 0, per_x) + sides * num_sent + side * num_sent + slot
    place = num_blocks + jnp.where(step_x == 0, (side - 1) * num_sent + slot, beyond_x)
    empty = num_blocks + sides * num_sent + 2 * per_x
    is_own = table < num_blocks
    is_empty = table >= num_blocks + 8 * num_sent
    place = jnp.where(is_own, table, place)
    dead = jnp.where(is_own, table >= count[0], is_empty | ~inside)
    dead = dead | (jnp.arange(num_blocks)[None] >= count[0])
    picks = jnp.where(dead, empty, place).astype(jnp.int32).reshape(-1)

    sent = to_rows(outgoing(sent_ids, count, blocks))
    beside = [lax.ppermute(sent, "sy", route) for route in along_y]
    column = jnp.concatenate([sent] + beside, axis=0)
    own_terms, *halo_terms = input_terms(
        picks, grads, weights, [num_sent] * sides + [per_x, per_x]
    )
    from_inner = lax.ppermute(column, "sx", inner)
    from_outer = lax.ppermute(column, "sx", outer)
    extended = [blocks] + [to_blocks(a) for a in beside + [from_inner, from_outer]]

    inner_back = lax.ppermute(to_rows(halo_terms[-2]), "sx", inner)
    outer_back = lax.ppermute(to_rows(halo_terms[-1]), "sx", outer)
    rows = num_sent * width
    returned = [inner_back[:rows], outer_back[:rows]]
    for number, route in enumerate(along_y):
        first, last = (1 + number) * rows, (2 + number) * rows
        portion = to_rows(halo_terms[number]) + inner_back[first:last] + outer_back[first:last]
        back = [(j, i) for i, j in route]
        returned.append(lax.ppermute(portion, "sy", back))

    scale = 1.0 / math.sqrt(num_blocks * width * size_z * size_x * size_y)
    if (size_z, size_x, size_y) == (4, 4, 2):
        me = (odd * 4 + (tile_x // 2) * 2 + tile_y).reshape(1)
        near, far = weight_terms(me, picks, grads, extended, offsets, scale, 8)

        def flat(z, x, y):
            return (z * size_x + x) * size_y + y

        def swap(array, dz, dx, dy):
            route = [
                (flat(z, x, y), flat(z ^ dz, x ^ dx, y ^ dy))
                for z in range(size_z)
                for x in range(size_x)
                for y in range(size_y)
            ]
            return lax.ppermute(array, AXES, route)

        near = near + swap(far, 0, 1, 0)
        shifts = ((0, 0, 1), (0, 2, 0), (0, 2, 1))
        part = near[0]
        for r, shift in enumerate(shifts):
            part = part + swap(near[r + 1], *shift)
        part = part + swap(part, 1, 0, 0)
        part = part + swap(part, 2, 0, 0)
        near = jnp.stack([part] + [swap(part, *shift) for shift in shifts])
        weight_grad = assemble(me, near, swap(near, 0, 1, 0)).reshape(weights.shape)
    else:
        zero = jnp.zeros((1,), jnp.int32)
        near, far = weight_terms(zero, picks, grads, extended, offsets, scale, 2)
        weight_grad = lax.psum(jnp.concatenate([near, far]).reshape(weights.shape), AXES)

    output = output_blocks(picks, weights, extended).reshape(features.shape)
    input_grad = input_grad_blocks(
        sent_ids, count, own_terms, [to_blocks(a) for a in returned]
    ).reshape(features.shape)
    return (output, input_grad, weight_grad)


def solution(mesh):
    tiles = P("dp", "sx", "sy", None, None)
    return jax.shard_map(
        local,
        mesh=mesh,
        in_specs=(tiles, tiles, P(), tiles, P("dp", "sx", "sy", None), P("dp", "sx", "sy")),
        out_specs=(tiles, tiles, P()),
        check_vma=False,
    )
```

time: 477 us -> 93.1 us (0.20)
  other arithmetic: 153 us -> 0.48 us
  waiting for transfers between devices: 127 us -> 28.5 us
  local copies, waits for them, and re-layouts: 81.9 us -> 5.08 us
  matrix products: 49.6 us -> 0 us
  Pallas kernels: 0 us -> 30.2 us
  between operations: 14.9 us -> 1.49 us
  starting transfers between devices: 39.3 us -> 27 us
  loops' own time: 7.98 us -> 0 us
    scatter-add x7 -> x0, other arithmetic: 139 us -> none  [the longest x6 138 us: grad_group(): accum.at[picks.reshape(-1)]]
    psum x1 -> x0, waiting for transfers between devices: 106 us -> none  [local(): weight_grad = lax.psum(scaled_part, ('dp', 'sx', 'sy'))]
    dot_general x18 -> x0, matrix products: 49.6 us -> none  [the longest x6 18.2 us: forward_group(): jnp.einsum('kgvc,kcd->gvd', gathered, weights, preferred_element_type=jnp...]
    pallas_call x0 -> x6, Pallas kernels: none -> 30.2 us  [the longest x1 9.85 us: input_terms(): pl.pallas_call(input_terms_kernel, out_shape=[jax.ShapeDtypeStruct((n, ro...]
    transpose x6 -> x0, local copies, waits for them, and re-layouts: 20.1 us -> none  [grad_group(): jnp.einsum('gvd,kcd->kgvc', grad_rows, weights, preferred_element_type=jn...]
    gather x7 -> x0, local copies, waits for them, and re-layouts: 17 us -> none  [the longest x6 16.4 us: forward_group(): gathered = extended[picks]]
    dynamic_slice x18 -> x0, local copies, waits for them, and re-layouts: 15.9 us -> none  [the longest x12 11.1 us: local(): lax.scan(grad_group, jnp.zeros((num_ext, width_block, channels), jnp.floa...]
    ppermute x16, starting transfers between devices: 39.3 us -> 27 us  [the longest x10 17.9 us: swap(): return lax.ppermute(array, AXES, route)]
  transfers between devices with their start and end apart: 17 -> 16, of which waited for: 6 -> 7; matrix products, arithmetic and copies ran while one was open for 57% -> 1% of each run, Pallas kernels for 0% -> 21%
where the time goes in v1:
time: 93.1 us; the launch traced here: 92.7 us
  Pallas kernels  30.2 us (32%)
  waiting for transfers between devices  28.5 us (31%)
  starting transfers between devices  27 us (29%)
  local copies, waits for them, and re-layouts  5.08 us (5%)
  between operations  1.49 us (2%)
    ppermute x10, waiting for transfers between devices, swap(): return lax.ppermute(array, AXES, route)  25 us
    ppermute x10, starting transfers between devices, swap(): return lax.ppermute(array, AXES, route)  17.9 us
    pallas_call x1, Pallas kernels, input_terms(): pl.pallas_call(input_terms_kernel, out_shape=[jax.ShapeDtypeStruct((n, ro...  9.85 us
    pallas_call x1, Pallas kernels, weight_terms(): pl.pallas_call(functools.partial(weight_terms_kernel, scale, chunks), out...  8.68 us
    pallas_call x1, Pallas kernels, output_blocks(): pl.pallas_call(functools.partial(output_kernel, 4), out_shape=jax.ShapeDt...  8.06 us
    unnamed x17, local copies, waits for them, and re-layouts  4.85 us
    ppermute x1, waiting for transfers between devices, local(): beside = [lax.ppermute(sent, 'sy', route) for route in along_y]  3.5 us
    ppermute x1, starting transfers between devices, local(): beside = [lax.ppermute(sent, 'sy', route) for route in along_y]  3.03 us
  transfers between devices with their start and end apart: 16, of which 7 were waited for; matrix products, arithmetic and copies ran while one was open for 1% of the time, Pallas kernels for 21%

profile of v1, /device:TPU:0, one launch (start us, length us, event | category | flops | bytes accessed | tf_op | source)
XLA Modules:
  0.0 92.7 jit_solution(12110407608848321401)
XLA Ops:
  1.3 1.1 %copy-done = bf16[1,1,1,3072,128]{4,3,2,1,0:T(8,128)(2,1)S(1)} copy-done((bf16[1,1,1,3072,128]{4,3,2,1,0:T(8,128)(2,1)S(1)}, bf16[1,1,1,3072,128]{4,3,2,1,0:T(8,128)(2,1)}, u32[]{:S(2)}) %copy-start) | copy-done | bytes 786456
  3.9 3.0 %collective-permute-start = (bf16[512,128]{1,0:T(8,128)(2,1)S(1)}, bf16[512,128]{1,0:T(8,128)(2,1)S(1)}, u32[]{:S(2)}, u32[]{:S(2)}) collective-permute-start(bf16[512,128]{1,0:T(8,128)(2,1)S(1)} %bitcast.47), channel_id=1, source_target_pairs={{0,1},{1,0},{2,3},{3,2},{4,5},{5,4},{6,7},{7,6},{8,9},{9,8},{10,11... | collective-permute-start | bytes 393224 | tf_op jit(solution)/shard_map/ppermute | solution.py:306
  6.9 3.5 %collective-permute-done = bf16[512,128]{1,0:T(8,128)(2,1)S(1)} collective-permute-done((bf16[512,128]{1,0:T(8,128)(2,1)S(1)}, bf16[512,128]{1,0:T(8,128)(2,1)S(1)}, u32[]{:S(2)}, u32[]{:S(2)}) %collective-permute-start) | collective-permute-done | bytes 131104 | tf_op jit(solution)/shard_map/ppermute | solution.py:306
  11.2 0.8 copy.9
  12.3 1.1 %copy-done.1 = bf16[1,1,1,3072,128]{4,3,2,1,0:T(8,128)(2,1)S(1)} copy-done((bf16[1,1,1,3072,128]{4,3,2,1,0:T(8,128)(2,1)S(1)}, bf16[1,1,1,3072,128]{4,3,2,1,0:T(8,128)(2,1)}, u32[]{:S(2)}) %copy-start.1) | copy-done | bytes 786456
  13.4 1.1 %copy-done.6 = bf16[1,1,1,3072,128]{4,3,2,1,0:T(8,128)(2,1)S(1)} copy-done((bf16[1,1,1,3072,128]{4,3,2,1,0:T(8,128)(2,1)S(1)}, bf16[1,1,1,3072,128]{4,3,2,1,0:T(8,128)(2,1)}, u32[]{:S(2)}) %copy-start.6) | copy-done | bytes 786456
  14.6 8.7 %shard_map.89 = (f32[4,432,128]{2,1,0:T(8,128)S(1)}, f32[4,432,128]{2,1,0:T(8,128)S(1)}) custom-call(s32[1]{0:T(128)} %bitcast.18.me_ref, s32[648]{0:T(1024)S(1)} %fusion.3.picks, bf16[3072,128]{1,0:T(8,128)(2,1)S(1)} %bitcast.57, bf16[24,128,128]{2,1,0:T(8,128)(2,1)S(1)} %bitcast.45, bf16[4,128,128]{2,1,0:T(8,128)(2,1)S(1)} %bitcast.51, ...), custom_call_target="tpu_custom_call" | custom-call | flops 10000000000 | bytes 4194304 | tf_op jit(solution)/shard_map/pallas_call | solution.py:139
  23.2 6.4 %collective-permute-start.6 = (f32[4,432,128]{2,1,0:T(8,128)S(1)}, f32[4,432,128]{2,1,0:T(8,128)S(1)}, u32[]{:S(2)}, u32[]{:S(2)}) collective-permute-start(f32[4,432,128]{2,1,0:T(8,128)S(1)} %get-tuple-element.14), channel_id=1, source_target_pairs={{0,2},{1,3},{2,0},{3,1},{4,6},{5,7},{6,4},{7,5},{8,10},{9,11},{10,... | collective-permute-start | bytes 2654216 | tf_op jit(solution)/shard_map/ppermute | solution.py:340
  29.7 2.1 %collective-permute-done.6 = f32[4,432,128]{2,1,0:T(8,128)S(1)} collective-permute-done((f32[4,432,128]{2,1,0:T(8,128)S(1)}, f32[4,432,128]{2,1,0:T(8,128)S(1)}, u32[]{:S(2)}, u32[]{:S(2)}) %collective-permute-start.6) | collective-permute-done | bytes 884768 | tf_op jit(solution)/shard_map/ppermute | solution.py:340
  31.9 2.6 %collective-permute-start.9 = (f32[432,128]{1,0:T(8,128)S(1)}, f32[432,128]{1,0:T(8,128)S(1)}, u32[]{:S(2)}, u32[]{:S(2)}) collective-permute-start(f32[432,128]{1,0:T(8,128)S(1)} %get-tuple-element.16), channel_id=1, source_target_pairs={{0,5},{1,4},{2,7},{3,6},{4,1},{5,0},{6,3},{7,2},{8,13},{9,12},{10,... | collective-permute-start | bytes 663560 | tf_op jit(solution)/shard_map/ppermute | solution.py:340
  35.5 9.8 %shard_map.87 = (f32[24,128,128]{2,1,0:T(8,128)S(1)}, f32[4,128,128]{2,1,0:T(8,128)S(1)}, f32[8,128,128]{2,1,0:T(8,128)S(1)}, f32[8,128,128]{2,1,0:T(8,128)S(1)}) custom-call(s32[648]{0:T(1024)S(1)} %fusion.3.picks, bf16[24,128,128]{2,1,0:T(8,128)(2,1)S(1)} %bitcast.58, bf16[3456,128]{1,0:T(8,128)(2,1)S(1)} %bitcast.55), custom_call_target="tpu_custom_call" | custom-call | flops 10000000000 | bytes 4194304 | tf_op jit(solution)/shard_map/pallas_call | solution.py:91
  46.1 3.0 %collective-permute-start.3 = (f32[1024,128]{1,0:T(8,128)S(1)}, f32[1024,128]{1,0:T(8,128)S(1)}, u32[]{:S(2)}, u32[]{:S(2)}) collective-permute-start(f32[1024,128]{1,0:T(8,128)S(1)} %bitcast.59), channel_id=1, source_target_pairs={{0,2},{2,0},{4,6},{6,4},{1,3},{3,1},{5,7},{7,5},{8,10},{10,8},{12,... | collective-permute-start | bytes 1572872 | tf_op jit(solution)/shard_map/ppermute | solution.py:315
  49.1 1.6 %collective-permute-start.10 = (f32[432,128]{1,0:T(8,128)S(1)}, f32[432,128]{1,0:T(8,128)S(1)}, u32[]{:S(2)}, u32[]{:S(2)}) collective-permute-start(f32[432,128]{1,0:T(8,128)S(1)} %fusion.2), channel_id=1, source_target_pairs={{0,8},{1,9},{2,10},{3,11},{4,12},{5,13},{6,14},{7,15},{8,0},{9,1},... | collective-permute-start | bytes 663560 | tf_op jit(solution)/shard_map/ppermute | solution.py:340
  50.8 5.8 %collective-permute-done.10 = f32[432,128]{1,0:T(8,128)S(1)} collective-permute-done((f32[432,128]{1,0:T(8,128)S(1)}, f32[432,128]{1,0:T(8,128)S(1)}, u32[]{:S(2)}, u32[]{:S(2)}) %collective-permute-start.10) | collective-permute-done | bytes 221216 | tf_op jit(solution)/shard_map/ppermute | solution.py:340
  56.6 2.7 %collective-permute-start.11 = (f32[432,128]{1,0:T(8,128)S(1)}, f32[432,128]{1,0:T(8,128)S(1)}, u32[]{:S(2)}, u32[]{:S(2)}) collective-permute-start(f32[432,128]{1,0:T(8,128)S(1)} %add.118), channel_id=1, source_target_pairs={{0,16},{1,17},{2,18},{3,19},{4,20},{5,21},{6,22},{7,23},{8,24},{9,... | collective-permute-start | bytes 663560 | tf_op jit(solution)/shard_map/ppermute | solution.py:340
  59.3 9.6 %collective-permute-done.11 = f32[432,128]{1,0:T(8,128)S(1)} collective-permute-done((f32[432,128]{1,0:T(8,128)S(1)}, f32[432,128]{1,0:T(8,128)S(1)}, u32[]{:S(2)}, u32[]{:S(2)}) %collective-permute-start.11) | collective-permute-done | bytes 221216 | tf_op jit(solution)/shard_map/ppermute | solution.py:340
  68.9 1.9 %collective-permute-start.14 = (f32[432,128]{1,0:T(8,128)S(1)}, f32[432,128]{1,0:T(8,128)S(1)}, u32[]{:S(2)}, u32[]{:S(2)}) collective-permute-start(f32[432,128]{1,0:T(8,128)S(1)} %add.119), channel_id=1, source_target_pairs={{0,5},{1,4},{2,7},{3,6},{4,1},{5,0},{6,3},{7,2},{8,13},{9,12},{10,... | collective-permute-start | bytes 663560 | tf_op jit(solution)/shard_map/ppermute | solution.py:340
  70.8 1.1 %collective-permute-start.13 = (f32[432,128]{1,0:T(8,128)S(1)}, f32[432,128]{1,0:T(8,128)S(1)}, u32[]{:S(2)}, u32[]{:S(2)}) collective-permute-start(f32[432,128]{1,0:T(8,128)S(1)} %add.119), channel_id=1, source_target_pairs={{0,4},{1,5},{2,6},{3,7},{4,0},{5,1},{6,2},{7,3},{8,12},{9,13},{10,... | collective-permute-start | bytes 663560 | tf_op jit(solution)/shard_map/ppermute | solution.py:340
  72.5 1.6 %collective-permute-start.5 = (f32[512,128]{1,0:T(8,128)S(1)}, f32[512,128]{1,0:T(8,128)S(1)}, u32[]{:S(2)}, u32[]{:S(2)}) collective-permute-start(f32[512,128]{1,0:T(8,128)S(1)} %get-tuple-element.18), channel_id=1, source_target_pairs={{1,0},{0,1},{3,2},{2,3},{5,4},{4,5},{7,6},{6,7},{9,8},{8,9},{11,10... | collective-permute-start | bytes 786440 | tf_op jit(solution)/shard_map/ppermute | solution.py:323
  74.1 4.1 %collective-permute-done.14 = f32[432,128]{1,0:T(8,128)S(1)} collective-permute-done((f32[432,128]{1,0:T(8,128)S(1)}, f32[432,128]{1,0:T(8,128)S(1)}, u32[]{:S(2)}, u32[]{:S(2)}) %collective-permute-start.14) | collective-permute-done | bytes 221216 | tf_op jit(solution)/shard_map/ppermute | solution.py:340
  78.2 2.7 %collective-permute-done.13 = f32[432,128]{1,0:T(8,128)S(1)} collective-permute-done((f32[432,128]{1,0:T(8,128)S(1)}, f32[432,128]{1,0:T(8,128)S(1)}, u32[]{:S(2)}, u32[]{:S(2)}) %collective-permute-start.13) | collective-permute-done | bytes 221216 | tf_op jit(solution)/shard_map/ppermute | solution.py:340
  81.8 8.1 %shard_map.86 = bf16[3072,128]{1,0:T(8,128)(2,1)} custom-call(s32[648]{0:T(1024)S(1)} %fusion.3.picks, bf16[3456,128]{1,0:T(8,128)(2,1)S(1)} %bitcast.56, bf16[24,128,128]{2,1,0:T(8,128)(2,1)S(1)} %bitcast.46, bf16[4,128,128]{2,1,0:T(8,128)(2,1)S(1)} %bitcast.52, bf16[8,128,128]{2,1,0:T(8,128)(2,1)S(1)} %bitcast.62, bf16[8,128,128]{2,1,0:T(8,128)(2,1)S(1)} %bitcast.64), custom_call_target="tpu_custom_call" | custom-call | flops 10000000000 | bytes 4194304 | tf_op jit(solution)/shard_map/pallas_call | solution.py:189
  89.9 1.6 %shard_map.88 = bf16[24,128,128]{2,1,0:T(8,128)(2,1)} custom-call(s32[4]{0:T(128)S(1)} %bitcast.54, s32[1]{0:T(128)} %bitcast.43.count_ref, f32[24,128,128]{2,1,0:T(8,128)S(1)} %get-tuple-element.9.own_ref, f32[4,128,128]{2,1,0:T(8,128)S(1)} %bitcast.49, f32[4,128,128]{2,1,0:T(8,128)S(1)} %bitcast.50, f32[4,128,128]{2,1,0:T(8,128)S(1)} %bitcast.65), custom_call_target="tpu_custom_call" | custom-call | flops 1000000000 | bytes 4194304 | tf_op jit(solution)/shard_map/pallas_call | solution.py:216
  91.4 1.3 %shard_map.90 = f32[8,432,128]{2,1,0:T(8,128)} custom-call(s32[1]{0:T(128)} %bitcast.18.me_ref, f32[4,432,128]{2,1,0:T(8,128)S(1)} %pad_maximum_fusion.near_ref, f32[4,432,128]{2,1,0:T(8,128)S(1)} %collective-permute-done.15.far_ref), custom_call_target="tpu_custom_call" | custom-call | tf_op jit(solution)/shard_map/pallas_call | solution.py:240
  (44 shorter events, 5.9 us)
Async XLA Ops:
  1.3 1.1 %copy-start = (bf16[1,1,1,3072,128]{4,3,2,1,0:T(8,128)(2,1)S(1)}, bf16[1,1,1,3072,128]{4,3,2,1,0:T(8,128)(2,1)}, u32[]{:S(2)}) copy-start(bf16[1,1,1,3072,128]{4,3,2,1,0:T(8,128)(2,1)} %param.6) | copy-start | bytes 2359300
  2.4 0.7 copy-start.3
  3.9 6.5 %collective-permute-start = (bf16[512,128]{1,0:T(8,128)(2,1)S(1)}, bf16[512,128]{1,0:T(8,128)(2,1)S(1)}, u32[]{:S(2)}, u32[]{:S(2)}) collective-permute-start(bf16[512,128]{1,0:T(8,128)(2,1)S(1)} %bitcast.47), channel_id=1, source_target_pairs={{0,1},{1,0},{2,3},{3,2},{4,5},{5,4},{6,7},{7,6},{8,9},{9,8},{10,11... | collective-permute-start | bytes 393224 | tf_op jit(solution)/shard_map/ppermute | solution.py:306
  10.4 1.9 %collective-permute-start.1 = (bf16[1024,128]{1,0:T(8,128)(2,1)S(1)}, bf16[1024,128]{1,0:T(8,128)(2,1)S(1)}, u32[]{:S(2)}, u32[]{:S(2)}) collective-permute-start(bf16[1024,128]{1,0:T(8,128)(2,1)S(1)} %pad_maximum_fusion.1), channel_id=1, source_target_pairs={{0,2},{2,0},{4,6},{6,4},{1,3},{3,1},{5,7},{7,5},{8,10},{10,8},{12,... | collective-permute-start | bytes 786440 | tf_op jit(solution)/shard_map/ppermute | solution.py:311
  10.5 1.8 %collective-permute-start.2 = (bf16[1024,128]{1,0:T(8,128)(2,1)S(1)}, bf16[1024,128]{1,0:T(8,128)(2,1)S(1)}, u32[]{:S(2)}, u32[]{:S(2)}) collective-permute-start(bf16[1024,128]{1,0:T(8,128)(2,1)S(1)} %pad_maximum_fusion.1), channel_id=1, source_target_pairs={{2,4},{4,2},{3,5},{5,3},{10,12},{12,10},{11,13},{13,11},{18,20},{2... | collective-permute-start | bytes 786440 | tf_op jit(solution)/shard_map/ppermute | solution.py:312
  12.3 1.1 %copy-start.1 = (bf16[1,1,1,3072,128]{4,3,2,1,0:T(8,128)(2,1)S(1)}, bf16[1,1,1,3072,128]{4,3,2,1,0:T(8,128)(2,1)}, u32[]{:S(2)}) copy-start(bf16[1,1,1,3072,128]{4,3,2,1,0:T(8,128)(2,1)} %param.6) | copy-start | bytes 2359300
  13.4 1.1 %copy-start.6 = (bf16[1,1,1,3072,128]{4,3,2,1,0:T(8,128)(2,1)S(1)}, bf16[1,1,1,3072,128]{4,3,2,1,0:T(8,128)(2,1)}, u32[]{:S(2)}) copy-start(bf16[1,1,1,3072,128]{4,3,2,1,0:T(8,128)(2,1)} %param.7) | copy-start | bytes 2359300
  23.2 8.5 %collective-permute-start.6 = (f32[4,432,128]{2,1,0:T(8,128)S(1)}, f32[4,432,128]{2,1,0:T(8,128)S(1)}, u32[]{:S(2)}, u32[]{:S(2)}) collective-permute-start(f32[4,432,128]{2,1,0:T(8,128)S(1)} %get-tuple-element.14), channel_id=1, source_target_pairs={{0,2},{1,3},{2,0},{3,1},{4,6},{5,7},{6,4},{7,5},{8,10},{9,11},{10,... | collective-permute-start | bytes 2654216 | tf_op jit(solution)/shard_map/ppermute | solution.py:340
  31.7 3.8 %copy-start.5 = (bf16[27,128,128]{2,1,0:T(8,128)(2,1)S(1)}, bf16[27,128,128]{2,1,0:T(8,128)(2,1)}, u32[]{:S(2)}) copy-start(bf16[27,128,128]{2,1,0:T(8,128)(2,1)} %param.8) | copy-start | bytes 2654212
  31.7 3.8 %copy-start.7 = (bf16[1,1,1,3072,128]{4,3,2,1,0:T(8,128)(2,1)S(1)}, bf16[1,1,1,3072,128]{4,3,2,1,0:T(8,128)(2,1)}, u32[]{:S(2)}) copy-start(bf16[1,1,1,3072,128]{4,3,2,1,0:T(8,128)(2,1)} %param.7) | copy-start | bytes 2359300
  31.9 17.1 %collective-permute-start.9 = (f32[432,128]{1,0:T(8,128)S(1)}, f32[432,128]{1,0:T(8,128)S(1)}, u32[]{:S(2)}, u32[]{:S(2)}) collective-permute-start(f32[432,128]{1,0:T(8,128)S(1)} %get-tuple-element.16), channel_id=1, source_target_pairs={{0,5},{1,4},{2,7},{3,6},{4,1},{5,0},{6,3},{7,2},{8,13},{9,12},{10,... | collective-permute-start | bytes 663560 | tf_op jit(solution)/shard_map/ppermute | solution.py:340
  34.6 14.5 %collective-permute-start.8 = (f32[432,128]{1,0:T(8,128)S(1)}, f32[432,128]{1,0:T(8,128)S(1)}, u32[]{:S(2)}, u32[]{:S(2)}) collective-permute-start(f32[432,128]{1,0:T(8,128)S(1)} %get-tuple-element.17), channel_id=1, source_target_pairs={{0,4},{1,5},{2,6},{3,7},{4,0},{5,1},{6,2},{7,3},{8,12},{9,13},{10,... | collective-permute-start | bytes 663560 | tf_op jit(solution)/shard_map/ppermute | solution.py:340
  35.2 13.8 %collective-permute-start.7 = (f32[432,128]{1,0:T(8,128)S(1)}, f32[432,128]{1,0:T(8,128)S(1)}, u32[]{:S(2)}, u32[]{:S(2)}) collective-permute-start(f32[432,128]{1,0:T(8,128)S(1)} %get-tuple-element.15), channel_id=1, source_target_pairs={{0,1},{1,0},{2,3},{3,2},{4,5},{5,4},{6,7},{7,6},{8,9},{9,8},{10,11... | collective-permute-start | bytes 663560 | tf_op jit(solution)/shard_map/ppermute | solution.py:340
  45.4 27.0 %collective-permute-start.4 = (f32[1024,128]{1,0:T(8,128)S(1)}, f32[1024,128]{1,0:T(8,128)S(1)}, u32[]{:S(2)}, u32[]{:S(2)}) collective-permute-start(f32[1024,128]{1,0:T(8,128)S(1)} %bitcast.60), channel_id=1, source_target_pairs={{2,4},{4,2},{3,5},{5,3},{10,12},{12,10},{11,13},{13,11},{18,20},{2... | collective-permute-start | bytes 1572872 | tf_op jit(solution)/shard_map/ppermute | solution.py:316
  46.1 26.3 %collective-permute-start.3 = (f32[1024,128]{1,0:T(8,128)S(1)}, f32[1024,128]{1,0:T(8,128)S(1)}, u32[]{:S(2)}, u32[]{:S(2)}) collective-permute-start(f32[1024,128]{1,0:T(8,128)S(1)} %bitcast.59), channel_id=1, source_target_pairs={{0,2},{2,0},{4,6},{6,4},{1,3},{3,1},{5,7},{7,5},{8,10},{10,8},{12,... | collective-permute-start | bytes 1572872 | tf_op jit(solution)/shard_map/ppermute | solution.py:315
  49.1 7.4 %collective-permute-start.10 = (f32[432,128]{1,0:T(8,128)S(1)}, f32[432,128]{1,0:T(8,128)S(1)}, u32[]{:S(2)}, u32[]{:S(2)}) collective-permute-start(f32[432,128]{1,0:T(8,128)S(1)} %fusion.2), channel_id=1, source_target_pairs={{0,8},{1,9},{2,10},{3,11},{4,12},{5,13},{6,14},{7,15},{8,0},{9,1},... | collective-permute-start | bytes 663560 | tf_op jit(solution)/shard_map/ppermute | solution.py:340
  56.6 12.2 %collective-permute-start.11 = (f32[432,128]{1,0:T(8,128)S(1)}, f32[432,128]{1,0:T(8,128)S(1)}, u32[]{:S(2)}, u32[]{:S(2)}) collective-permute-start(f32[432,128]{1,0:T(8,128)S(1)} %add.118), channel_id=1, source_target_pairs={{0,16},{1,17},{2,18},{3,19},{4,20},{5,21},{6,22},{7,23},{8,24},{9,... | collective-permute-start | bytes 663560 | tf_op jit(solution)/shard_map/ppermute | solution.py:340
  68.9 9.3 %collective-permute-start.14 = (f32[432,128]{1,0:T(8,128)S(1)}, f32[432,128]{1,0:T(8,128)S(1)}, u32[]{:S(2)}, u32[]{:S(2)}) collective-permute-start(f32[432,128]{1,0:T(8,128)S(1)} %add.119), channel_id=1, source_target_pairs={{0,5},{1,4},{2,7},{3,6},{4,1},{5,0},{6,3},{7,2},{8,13},{9,12},{10,... | collective-permute-start | bytes 663560 | tf_op jit(solution)/shard_map/ppermute | solution.py:340
  70.8 10.2 %collective-permute-start.13 = (f32[432,128]{1,0:T(8,128)S(1)}, f32[432,128]{1,0:T(8,128)S(1)}, u32[]{:S(2)}, u32[]{:S(2)}) collective-permute-start(f32[432,128]{1,0:T(8,128)S(1)} %add.119), channel_id=1, source_target_pairs={{0,4},{1,5},{2,6},{3,7},{4,0},{5,1},{6,2},{7,3},{8,12},{9,13},{10,... | collective-permute-start | bytes 663560 | tf_op jit(solution)/shard_map/ppermute | solution.py:340
  71.9 9.7 %collective-permute-start.12 = (f32[432,128]{1,0:T(8,128)S(1)}, f32[432,128]{1,0:T(8,128)S(1)}, u32[]{:S(2)}, u32[]{:S(2)}) collective-permute-start(f32[432,128]{1,0:T(8,128)S(1)} %add.119), channel_id=1, source_target_pairs={{0,1},{1,0},{2,3},{3,2},{4,5},{5,4},{6,7},{7,6},{8,9},{9,8},{10,11... | collective-permute-start | bytes 663560 | tf_op jit(solution)/shard_map/ppermute | solution.py:340
  72.4 9.4 %copy-start.2 = (bf16[1,1,1,3072,128]{4,3,2,1,0:T(8,128)(2,1)S(1)}, bf16[1,1,1,3072,128]{4,3,2,1,0:T(8,128)(2,1)}, u32[]{:S(2)}) copy-start(bf16[1,1,1,3072,128]{4,3,2,1,0:T(8,128)(2,1)} %param.6) | copy-start | bytes 2359300
  72.5 17.4 %collective-permute-start.5 = (f32[512,128]{1,0:T(8,128)S(1)}, f32[512,128]{1,0:T(8,128)S(1)}, u32[]{:S(2)}, u32[]{:S(2)}) collective-permute-start(f32[512,128]{1,0:T(8,128)S(1)} %get-tuple-element.18), channel_id=1, source_target_pairs={{1,0},{0,1},{3,2},{2,3},{5,4},{4,5},{7,6},{6,7},{9,8},{8,9},{11,10... | collective-permute-start | bytes 786440 | tf_op jit(solution)/shard_map/ppermute | solution.py:323
  81.7 8.2 %copy-start.4 = (s32[1,1,1,4]{3,2,1,0:T(1,128)S(1)}, s32[1,1,1,4]{3,2,1,0:T(1,128)}, u32[]{:S(2)}) copy-start(s32[1,1,1,4]{3,2,1,0:T(1,128)} %param.10) | copy-start | bytes 52
  81.7 9.7 %collective-permute-start.15 = (f32[4,432,128]{2,1,0:T(8,128)S(1)}, f32[4,432,128]{2,1,0:T(8,128)S(1)}, u32[]{:S(2)}, u32[]{:S(2)}) collective-permute-start(f32[4,432,128]{2,1,0:T(8,128)S(1)} %pad_maximum_fusion.near_ref), channel_id=1, source_target_pairs={{0,2},{1,3},{2,0},{3,1},{4,6},{5,7},{6,4},{7,5},{8,10},{9,11},{10,... | collective-permute-start | bytes 2654216 | tf_op jit(solution)/shard_map/ppermute | solution.py:340

commit v2 on v1

v2 whole, which is shorter than its diff:
```python
import functools
import math

import jax
import jax.numpy as jnp
from jax import lax
from jax.experimental import pallas as pl
from jax.experimental.pallas import tpu as pltpu
from jax.sharding import PartitionSpec as P

AXES = ("dp", "sx", "sy")
F32 = jnp.float32
BF16 = jnp.bfloat16
VMEM = pl.BlockSpec(memory_space=pltpu.VMEM)
SMEM = pl.BlockSpec(memory_space=pltpu.SMEM)
ANY = pl.BlockSpec(memory_space=pl.ANY)
HBM = pl.BlockSpec(memory_space=pltpu.HBM)


def params():
    return pltpu.CompilerParams(vmem_limit_bytes=12 * 2**20)


def cost(flops):
    return pl.CostEstimate(flops=flops, bytes_accessed=2**16, transcendentals=0)


def outgoing_kernel(sent_ref, count_ref, x_ref, out_ref, sems):
    num_sent = out_ref.shape[0]
    copies = [
        pltpu.make_async_copy(x_ref.at[sent_ref[s]], out_ref.at[s], sems.at[s])
        for s in range(num_sent)
    ]
    for copy in copies:
        copy.start()
    for copy in copies:
        copy.wait()
    for s in range(num_sent):

        @pl.when(sent_ref[s] >= count_ref[0])
        def _():
            out_ref[s] = jnp.zeros(out_ref.shape[1:], out_ref.dtype)


def outgoing(sent_ids, count, blocks):
    num_sent = sent_ids.shape[0]
    return pl.pallas_call(
        outgoing_kernel,
        out_shape=jax.ShapeDtypeStruct((num_sent,) + blocks.shape[1:], blocks.dtype),
        in_specs=[SMEM, SMEM, HBM],
        out_specs=VMEM,
        scratch_shapes=[pltpu.SemaphoreType.DMA((num_sent,))],
        compiler_params=params(),
        cost_estimate=pl.CostEstimate(flops=0, bytes_accessed=2**18, transcendentals=0),
    )(sent_ids, count, pltpu.with_memory_space_constraint(blocks, pltpu.HBM))


def input_terms_kernel(halo_spans, picks, grad_ref, weight_ref, own_ref, *rest):
    *halo_refs, accum = rest
    num_blocks, rows, channels = grad_ref.shape
    offsets = weight_ref.shape[0] // channels
    accum[...] = jnp.zeros_like(accum)

    def term(o, matrix):
        return lax.dot_general(
            grad_ref[o], matrix, (((1,), (1,)), ((), ())), preferred_element_type=F32
        )

    def two_offsets(pair, carry):
        start = pl.multiple_of(pair * 2 * channels, 2 * channels)
        matrix = weight_ref[pl.ds(start, 2 * channels), :]
        for o in range(num_blocks):
            both = term(o, matrix)
            accum[picks[o, 2 * pair]] += both[:, :channels]
            accum[picks[o, 2 * pair + 1]] += both[:, channels:]
        return carry

    lax.fori_loop(0, offsets // 2, two_offsets, 0)
    if offsets % 2:
        matrix = weight_ref[(offsets - 1) * channels :, :]
        for o in range(num_blocks):
            accum[picks[o, offsets - 1]] += term(o, matrix)
    own_ref[...] = accum[:num_blocks]
    for ref, spans in zip(halo_refs, halo_spans):
        to = 0
        for start, size in spans:
            ref[to : to + size] = accum[num_blocks + start : num_blocks + start + size]
            to += size


def input_terms(picks, grad, weights, halo_spans):
    num_blocks, rows, channels = grad.shape
    sizes = [num_blocks] + [sum(size for _, size in spans) for spans in halo_spans]
    return pl.pallas_call(
        functools.partial(input_terms_kernel, halo_spans),
        out_shape=[jax.ShapeDtypeStruct((n, rows, channels), F32) for n in sizes],
        in_specs=[SMEM, VMEM, VMEM],
        out_specs=[VMEM] * len(sizes),
        scratch_shapes=[pltpu.VMEM((sum(sizes) + 1, rows, channels), F32)],
        compiler_params=params(),
        cost_estimate=cost(10**7),
    )(picks, grad, weights.reshape(-1, channels))


def turn_kernel(block_ref, grad_ref, turned_ref, copy_ref):
    for e in range(block_ref.shape[0]):
        turned_ref[e] = block_ref[e].T
    copy_ref[...] = grad_ref[...]


def turn(blocks, grad):
    num_blocks, rows, channels = blocks.shape
    return pl.pallas_call(
        turn_kernel,
        out_shape=[
            jax.ShapeDtypeStruct((num_blocks, channels, rows), BF16),
            jax.ShapeDtypeStruct(grad.shape, BF16),
        ],
        in_specs=[VMEM, VMEM],
        out_specs=[VMEM, VMEM],
        compiler_params=params(),
        cost_estimate=cost(10**7),
    )(blocks, grad)


def weight_terms_kernel(scale, group, order_ref, picks, grad_ref, *rest):
    own_ref, *block_refs, out_ref, turned = rest
    channels = grad_ref.shape[1]
    rows = own_ref.shape[2]
    num_blocks = grad_ref.shape[0] // rows
    chunks, slots, size = out_ref.shape[:3]
    offsets = slots - 1
    start = own_ref.shape[0]
    turned[:start] = own_ref[...]
    for ref in block_refs:
        for e in range(ref.shape[0]):
            turned[start + e] = ref[e].T
        start += ref.shape[0]
    turned[start] = jnp.zeros(turned.shape[1:], turned.dtype)
    half = chunks * size
    lowest = order_ref[0]
    for r in range(1, chunks):
        lowest = jnp.minimum(lowest, order_ref[r])
    part = pl.ds(pl.multiple_of(lowest * size, half), half)

    def some_offsets(index, peak):
        wide = []
        for j in range(group):
            gathered = [turned[picks[o, index * group + j], part] for o in range(num_blocks)]
            wide.append(jnp.concatenate(gathered, axis=1))
        terms = jnp.dot(
            jnp.concatenate(wide, axis=0), grad_ref[...], preferred_element_type=F32
        )
        terms = (terms * scale).reshape(group, chunks, size, channels)
        for r in range(chunks):
            out_ref[order_ref[chunks + r], pl.ds(index * group, group)] = terms[:, r]
        return jnp.maximum(peak, jnp.max(jnp.abs(terms).reshape(-1, 8, channels), axis=0))

    peak = lax.fori_loop(
        0, offsets // group, some_offsets, jnp.zeros((8, channels), F32)
    )
    out_ref[:, offsets] = jnp.broadcast_to(jnp.max(peak), (chunks, size, channels))


def weight_terms(order, picks, grad, blocks, offsets, scale, chunks):
    num_blocks, rows, channels = grad.shape
    total = sum(b.shape[0] for b in blocks) + 1
    group = next(g for g in (9, 3, 1) if offsets % g == 0)
    size = channels // 8
    return pl.pallas_call(
        functools.partial(weight_terms_kernel, scale, group),
        out_shape=jax.ShapeDtypeStruct((chunks, offsets + 1, size, channels), F32),
        in_specs=[SMEM, SMEM, VMEM] + [VMEM] * len(blocks),
        out_specs=VMEM,
        scratch_shapes=[pltpu.VMEM((total, channels, rows), BF16)],
        compiler_params=params(),
        cost_estimate=cost(10**7),
    )(order, picks, grad.reshape(-1, channels), *blocks)


def output_kernel(group, span, done, picks, weight_ref, *rest):
    *block_refs, out_ref, held = rest
    if done:
        done_ref, *block_refs = block_refs
        out_ref[: done_ref.shape[0], :] = done_ref[...]
    total, rows, channels = held.shape
    offsets = weight_ref.shape[0] // channels
    start = 0
    for ref in block_refs:
        held[start : start + ref.shape[0]] = ref[...]
        start += ref.shape[0]
    held[start] = jnp.zeros(held.shape[1:], held.dtype)

    def some_blocks(index, carry):
        accum = jnp.zeros((group * rows, channels), F32)
        for k in range(0, offsets, 2):
            pair = range(k, min(k + 2, offsets))
            gathered = [
                jnp.concatenate(
                    [held[picks[index * group + j, kk]] for kk in pair], axis=1
                )
                for j in range(group)
            ]
            accum += jnp.dot(
                jnp.concatenate(gathered, axis=0),
                weight_ref[k * channels : (k + len(pair)) * channels, :],
                preferred_element_type=F32,
            )
        first = pl.multiple_of(index * group * rows, group * rows)
        out_ref[pl.ds(first, group * rows), :] = accum.astype(BF16)
        return carry

    lax.fori_loop(span[0] // group, span[1] // group, some_blocks, 0)


def output_blocks(picks, weights, blocks, span, done=()):
    _, rows, channels = blocks[0].shape
    total = sum(b.shape[0] for b in blocks) + 1
    group = next(g for g in (8, 6, 4, 2, 1) if span[0] % g == span[1] % g == 0)
    return pl.pallas_call(
        functools.partial(output_kernel, group, span, len(done)),
        out_shape=jax.ShapeDtypeStruct((span[1] * rows, channels), BF16),
        in_specs=[SMEM, VMEM] + [VMEM] * (len(done) + len(blocks)),
        out_specs=VMEM,
        scratch_shapes=[pltpu.VMEM((total, rows, channels), BF16)],
        compiler_params=params(),
        cost_estimate=cost(10**7),
    )(picks, weights.reshape(-1, channels), *done, *blocks)


def input_grad_kernel(sent_ref, count_ref, own_ref, *rest):
    *returned_refs, out_ref = rest
    num_blocks = own_ref.shape[0]
    for b in range(num_blocks):
        keep = jnp.where(b < count_ref[0], 1.0, 0.0)
        out_ref[b] = (own_ref[b] * keep).astype(BF16)
    for s in range(returned_refs[0].shape[0]):
        b = sent_ref[s]
        keep = jnp.where(b < count_ref[0], 1.0, 0.0)
        returned = returned_refs[0][s]
        for ref in returned_refs[1:]:
            returned = returned + ref[s]
        out_ref[b] = ((own_ref[b] + returned) * keep).astype(BF16)


def input_grad_blocks(sent_ids, count, own, returned):
    return pl.pallas_call(
        input_grad_kernel,
        out_shape=jax.ShapeDtypeStruct(own.shape, BF16),
        in_specs=[SMEM, SMEM, VMEM] + [VMEM] * len(returned),
        out_specs=VMEM,
        compiler_params=params(),
        cost_estimate=cost(10**7),
    )(sent_ids, count, own, *returned)


def assemble_kernel(order_ref, *rest):
    *piece_refs, out_ref, sems = rest
    chunks = [ref.at[r] for ref in piece_refs for r in range(ref.shape[0])]
    size = chunks[0].shape[1]
    copies = []
    for r, chunk in enumerate(chunks):
        first = pl.multiple_of(order_ref[r] * size, size)
        copies.append(
            pltpu.make_async_copy(
                chunk.at[: out_ref.shape[0]], out_ref.at[:, pl.ds(first, size)], sems.at[r]
            )
        )
    for copy in copies:
        copy.start()
    for copy in copies:
        copy.wait()


def assemble(order, pieces):
    count = sum(p.shape[0] for p in pieces)
    _, slots, size, channels = pieces[0].shape
    return pl.pallas_call(
        assemble_kernel,
        out_shape=jax.ShapeDtypeStruct((slots - 1, count * size, channels), F32),
        in_specs=[SMEM] + [ANY] * len(pieces),
        out_specs=ANY,
        scratch_shapes=[pltpu.SemaphoreType.DMA((count,))],
        compiler_params=params(),
    )(order, *pieces)


def local(features, cotangent, weights, tables, send_lists, counts):
    num_blocks = tables.shape[4]
    num_sent = send_lists.shape[3]
    offsets, channels = weights.shape[0], weights.shape[1]
    width = features.shape[3] // num_blocks
    size_z, size_x, size_y = (lax.axis_size(a) for a in AXES)
    scene, tile_x, tile_y = (lax.axis_index(a) for a in AXES)
    blocks = features.reshape(num_blocks, width, channels)
    grads = cotangent.reshape(num_blocks, width, channels)
    sent_ids = send_lists.reshape(num_sent)
    count = counts.reshape(1)

    odd = tile_x % 2
    inner = [(i, i ^ 1) for i in range(size_x) if (i ^ 1) < size_x]
    outer = [(i, i + 1) for i in range(1, size_x - 1, 2)]
    outer = outer + [(j, i) for i, j in outer]
    if size_y == 2:
        along_y = [[(0, 1), (1, 0)]]
    else:
        along_y = [
            [(i, i + 1) for i in range(size_y - 1)],
            [(i + 1, i) for i in range(size_y - 1)],
        ]
    sides = len(along_y)
    per_x = (1 + sides) * num_sent
    paired = (size_z, size_x, size_y) == (4, 4, 2)

    def to_blocks(array):
        return array.reshape(-1, width, channels)

    def to_rows(array):
        return array.reshape(-1, channels)

    table = tables.reshape(offsets, num_blocks).T
    code = table - num_blocks
    number = code // num_sent
    cell = number + (number >= 4)
    step_x, step_y = cell // 3 - 1, cell % 3 - 1
    slot = code % num_sent
    near_x, near_y = tile_x + step_x, tile_y + step_y
    inside = (near_x >= 0) & (near_x < size_x) & (near_y >= 0) & (near_y < size_y)
    if size_y == 2:
        side = (step_y != 0).astype(jnp.int32)
    else:
        side = jnp.where(step_y == 0, 0, jnp.where(step_y < 0, 1, 2))
    toward = 1 - 2 * odd
    if paired:
        middle = (tile_x == 1) | (tile_x == 2)
        to_inner = jnp.where(side == 0, 0, jnp.where(middle, 3, 2))
        place = jnp.where(
            step_x == 0, jnp.where(middle, 4, 1), jnp.where(step_x == toward, to_inner, 1 + side)
        )
        place = num_blocks + place * num_sent + slot
        empty = num_blocks + 5 * num_sent
    else:
        beyond_x = jnp.where(step_x == toward, 0, per_x) + (sides + side) * num_sent + slot
        place = num_blocks + jnp.where(step_x == 0, (side - 1) * num_sent + slot, beyond_x)
        empty = num_blocks + sides * num_sent + 2 * per_x
    is_own = table < num_blocks
    is_empty = table >= num_blocks + 8 * num_sent
    place = jnp.where(is_own, table, place)
    dead = jnp.where(is_own, table >= count[0], is_empty | ~inside)
    dead = dead | (jnp.arange(num_blocks)[:, None] >= count[0])
    picks = jnp.where(dead, empty, place).astype(jnp.int32)

    sent = to_rows(outgoing(sent_ids, count, blocks))
    turned_own, kept_grads = turn(blocks, grads)
    scale = 1.0 / math.sqrt(num_blocks * width * size_z * size_x * size_y)
    if paired:

        def flat(z, x, c, y):
            return (z * size_x + 2 * x + c) * size_y + y

        def exchange(array, to, senders=lambda z, x, c, y: True):
            places = [
                (z, x, c, y) for z in range(4) for x in range(2) for c in range(2) for y in range(2)
            ]
            route = [(flat(*p), flat(*to(*p))) for p in places if senders(*p)]
            return lax.ppermute(array, AXES, route)

        def cores(z, x, c, y):
            return z, x, 1 - c, y

        def is_middle(z, x, c, y):
            return x != c

        def straight(z, x, c, y):
            return (z, 1 - x, 1 - c, y) if is_middle(z, x, c, y) else (z, x, c, 1 - y)

        def across(z, x, c, y):
            return (z, 1 - x, 1 - c, 1 - y) if is_middle(z, x, c, y) else (z, x, c, 1 - y)

        def is_end(*p):
            return not is_middle(*p)

        beside = exchange(sent, cores)
        first = exchange(sent, straight)
        second = exchange(jnp.where(middle, sent, beside), across)
        first, second, turned_own = lax.optimization_barrier((first, second, turned_own))
        passed = [exchange(first, cores, is_end), exchange(second, cores, is_end)]
        extended = [blocks] + [to_blocks(a) for a in [beside, first, second] + passed]

        core, far_x = odd, tile_x // 2
        chunk = jnp.arange(4, dtype=jnp.int32)
        low = far_x * 2 + tile_y
        swapped = (chunk % 2) * 2 + chunk // 2
        mine = jnp.where(core == 0, chunk, swapped)
        theirs = jnp.where(core == 0, swapped, chunk)
        keep, send = core * 4 + (low ^ mine), (1 - core) * 4 + (low ^ theirs)

        def places(bits):
            moved = chunk ^ low
            return jnp.where(bits == 0, moved, (moved % 2) * 2 + moved // 2)

        near_order = jnp.concatenate([core * 4 + chunk, places(core)])
        far_order = jnp.concatenate([(1 - core) * 4 + chunk, places(1 - core)])
        order = jnp.concatenate([keep, send])
        blocks_turned = [turned_own] + extended[1:]
        far = weight_terms(far_order, picks, kept_grads, blocks_turned, offsets, scale, 4)
        kept_grads, far = lax.optimization_barrier((kept_grads, far))
        near = weight_terms(near_order, picks, kept_grads, blocks_turned, offsets, scale, 4)

        def x_or_y(z, x, c, y):
            return (z, 1 - x, c, y) if c == 0 else (z, x, c, 1 - y)

        def y_or_x(z, x, c, y):
            return (z, x, c, 1 - y) if c == 0 else (z, 1 - x, c, y)

        def z_far(z, x, c, y):
            return (z ^ 2, x, c, y)

        def z_near(z, x, c, y):
            return (z ^ 1, x, c, y)

        slot_id = lax.broadcasted_iota(jnp.int32, (1, offsets + 1, 1, 1), 1)

        def encode(part):
            bound = jnp.maximum(part[:, offsets:], 1e-30)
            exponent = jnp.ceil(jnp.log2(bound)) - 15.0
            values = part * jnp.exp2(-exponent)
            return jnp.where(slot_id < offsets, values, exponent).astype(jnp.float16)

        def decode(message):
            wide = message.astype(F32)
            unit = jnp.exp2(wide[:, offsets:])
            return jnp.where(slot_id < offsets, wide * unit, unit * 32768.0)

        near = near + exchange(far, cores)
        message, pair = encode(near[2:]), near[:2]
        message, pair, late_grads = lax.optimization_barrier((message, pair, kept_grads))
        spans = [(r * num_sent, num_sent) for r in range(5)]
        own_terms, inner_terms, first_terms, second_terms = input_terms(
            picks, late_grads, weights, [[spans[0], spans[3], spans[4]], [spans[1]], [spans[2]]]
        )
        back = exchange(inner_terms, cores)
        pair = pair + decode(exchange(message, x_or_y))
        message, part, own_terms, late_picks = lax.optimization_barrier(
            (encode(pair[1:]), pair[:1], own_terms, picks)
        )
        middle_block = num_blocks // 2
        upper = output_blocks(late_picks, weights, extended, (0, middle_block))
        message = encode(part + decode(exchange(message, y_or_x)))
        message, back, upper = lax.optimization_barrier((message, back, upper))
        first_back = exchange(first_terms + back[num_sent : 2 * num_sent], straight)
        second_back = exchange(second_terms + back[2 * num_sent :], across)
        part = decode(message) + decode(exchange(message, z_far))
        message, late_picks, first_back, second_back = lax.optimization_barrier(
            (encode(part), late_picks, first_back, second_back)
        )
        output = output_blocks(
            late_picks, weights, extended, (middle_block, num_blocks), (upper,)
        )
        passed_back = exchange(second_back, cores, is_end)
        part = decode(message) + decode(exchange(message, z_near))
        returned = [
            back[:num_sent] + jnp.where(middle, second_back, 0.0),
            first_back,
            passed_back,
        ]
        message, output, own_terms = lax.optimization_barrier((encode(part), output, own_terms))
        input_grad = input_grad_blocks(sent_ids, count, own_terms, returned)
        pair = jnp.concatenate([message, exchange(message, y_or_x)])
        pair, input_grad = lax.optimization_barrier((pair, input_grad))
        rest = exchange(pair, x_or_y)
        messages = [pair, rest, exchange(pair, cores), exchange(rest, cores)]
        weight_grad = assemble(order, [decode(m) for m in messages])

    else:
        beside = [lax.ppermute(sent, "sy", route) for route in along_y]
        column = jnp.concatenate([sent] + beside, axis=0)
        from_inner = lax.ppermute(column, "sx", inner)
        from_outer = lax.ppermute(column, "sx", outer)
        extended = [blocks] + [to_blocks(a) for a in beside + [from_inner, from_outer]]
        order = jnp.concatenate([jnp.arange(8, dtype=jnp.int32)] * 2)
        parts = weight_terms(
            order, picks, kept_grads, [turned_own] + extended[1:], offsets, scale, 8
        )
        parts = jnp.swapaxes(parts[:, :offsets], 0, 1)
        weight_grad = lax.psum(parts.reshape(weights.shape), AXES)

        spans = [(r * num_sent, num_sent) for r in range(sides)]
        spans += [(sides * num_sent + r * per_x, per_x) for r in range(2)]
        own_terms, *halo_terms = input_terms(picks, grads, weights, [[span] for span in spans])
        inner_back = lax.ppermute(halo_terms[-2], "sx", inner)
        outer_back = lax.ppermute(halo_terms[-1], "sx", outer)
        returned = [inner_back[:num_sent], outer_back[:num_sent]]
        for number, route in enumerate(along_y):
            part = slice((1 + number) * num_sent, (2 + number) * num_sent)
            portion = halo_terms[number] + inner_back[part] + outer_back[part]
            returned.append(lax.ppermute(portion, "sy", [(j, i) for i, j in route]))
        output = output_blocks(picks, weights, extended, (0, num_blocks))
        input_grad = input_grad_blocks(sent_ids, count, own_terms, returned)

    return (output.reshape(features.shape), input_grad.reshape(features.shape), weight_grad)


def solution(mesh):
    tiles = P("dp", "sx", "sy", None, None)
    return jax.shard_map(
        local,
        mesh=mesh,
        in_specs=(tiles, tiles, P(), tiles, P("dp", "sx", "sy", None), P("dp", "sx", "sy")),
        out_specs=(tiles, tiles, P()),
        check_vma=False,
    )
```

time: 93.1 us -> 84.8 us (0.911)
  starting transfers between devices: 27 us -> 18.6 us
  waiting for transfers between devices: 28.5 us -> 24.6 us
  other arithmetic: 0.48 us -> 4.24 us
  local copies, waits for them, and re-layouts: 5.08 us -> 1.79 us
  Pallas kernels: 30.2 us -> 33.4 us
    ppermute x16 -> x18, starting transfers between devices: 27 us -> 18.6 us  [exchange(): return lax.ppermute(array, AXES, route)]
    ppermute x16 -> x18, waiting for transfers between devices: 28.5 us -> 24.6 us  [exchange(): return lax.ppermute(array, AXES, route)]
    unnamed x17 -> x10, local copies, waits for them, and re-layouts: 4.85 us -> 1.79 us
    pallas_call x4 -> x7, Pallas kernels: 27.9 us -> 30.5 us  [the longest x1 10 us: input_terms(): pl.pallas_call(functools.partial(input_terms_kernel, halo_spans), out_sha...]
    add x5 -> x10, other arithmetic: 0.37 us -> 1.92 us  [the longest x1 1.37 us: local(): near = near + exchange(far, cores)]
    select_n x1 -> x4, other arithmetic: 0.03 us -> 1.07 us  [the longest x1 0.78 us: local(): picks = jnp.where(dead, empty, place).astype(jnp.int32)]
  transfers between devices with their start and end apart: 16 -> 18, of which waited for: 7 -> 8; matrix products, arithmetic and copies ran while one was open for 1% -> 3% of each run, Pallas kernels for 21% -> 28%
where the time goes in v2:
time: 84.8 us; the launch traced here: 84.4 us
  Pallas kernels  33.4 us (39%)
  waiting for transfers between devices  24.6 us (29%)
  starting transfers between devices  18.6 us (22%)
  other arithmetic  4.24 us (5%)
  between operations  1.8 us (2%)
  local copies, waits for them, and re-layouts  1.79 us (2%)
    ppermute x18, waiting for transfers between devices, exchange(): return lax.ppermute(array, AXES, route)  24.6 us
    ppermute x18, starting transfers between devices, exchange(): return lax.ppermute(array, AXES, route)  18.6 us
    pallas_call x1, Pallas kernels, input_terms(): pl.pallas_call(functools.partial(input_terms_kernel, halo_spans), out_sha...  10 us
    pallas_call x2, Pallas kernels, weight_terms(): pl.pallas_call(functools.partial(weight_terms_kernel, scale, group), out_...  9.62 us
    pallas_call x2, Pallas kernels, output_blocks(): pl.pallas_call(functools.partial(output_kernel, group, span, len(done)),...  8.76 us
    pallas_call x1, Pallas kernels, assemble(): pl.pallas_call(assemble_kernel, out_shape=jax.ShapeDtypeStruct((slots - 1...  1.81 us
    unnamed x10, local copies, waits for them, and re-layouts  1.79 us
  transfers between devices with their start and end apart: 18, of which 8 were waited for; matrix products, arithmetic and copies ran while one was open for 3% of the time, Pallas kernels for 28%

profile of v2, /device:TPU:0, one launch (start us, length us, event | category | flops | bytes accessed | tf_op | source)
XLA Modules:
  0.0 84.4 jit_solution(15504198528404663330)
XLA Ops:
  2.0 1.4 %shard_map.86 = bf16[4,128,128]{2,1,0:T(8,128)(2,1)S(1)} custom-call(s32[4]{0:T(128)S(1)} %bitcast.131, s32[1]{0:T(128)} %bitcast.97.count_ref, bf16[24,128,128]{2,1,0:T(8,128)(2,1)} %bitcast.99), custom_call_target="tpu_custom_call" | custom-call | bytes 262144 | tf_op jit(solution)/shard_map/pallas_call | solution.py:47
  3.9 2.6 %collective-permute-start = (bf16[512,128]{1,0:T(8,128)(2,1)S(1)}, bf16[512,128]{1,0:T(8,128)(2,1)S(1)}, u32[]{:S(2)}, u32[]{:S(2)}) collective-permute-start(bf16[512,128]{1,0:T(8,128)(2,1)S(1)} %bitcast.130), channel_id=1, source_target_pairs={{0,1},{1,0},{2,4},{3,5},{4,2},{5,3},{6,7},{7,6},{8,9},{9,8},{10,12... | collective-permute-start | bytes 393224 | tf_op jit(solution)/shard_map/ppermute | solution.py:366
  6.6 1.3 %collective-permute-start.2 = (bf16[512,128]{1,0:T(8,128)(2,1)S(1)}, bf16[512,128]{1,0:T(8,128)(2,1)S(1)}, u32[]{:S(2)}, u32[]{:S(2)}) collective-permute-start(bf16[512,128]{1,0:T(8,128)(2,1)S(1)} %broadcast_select_fusion), channel_id=1, source_target_pairs={{0,1},{1,0},{2,5},{3,4},{4,3},{5,2},{6,7},{7,6},{8,9},{9,8},{10,13... | collective-permute-start | bytes 393224 | tf_op jit(solution)/shard_map/ppermute | solution.py:366
  10.1 2.9 %collective-permute-done.2 = bf16[512,128]{1,0:T(8,128)(2,1)S(1)} collective-permute-done((bf16[512,128]{1,0:T(8,128)(2,1)S(1)}, bf16[512,128]{1,0:T(8,128)(2,1)S(1)}, u32[]{:S(2)}, u32[]{:S(2)}) %collective-permute-start.2) | collective-permute-done | bytes 131104 | tf_op jit(solution)/shard_map/ppermute | solution.py:366
  13.0 1.3 %collective-permute-start.3 = (bf16[512,128]{1,0:T(8,128)(2,1)S(1)}, bf16[512,128]{1,0:T(8,128)(2,1)S(1)}, u32[]{:S(2)}, u32[]{:S(2)}) collective-permute-start(bf16[512,128]{1,0:T(8,128)(2,1)S(1)} %collective-permute-done), channel_id=1, source_target_pairs={{0,2},{1,3},{6,4},{7,5},{8,10},{9,11},{14,12},{15,13},{16,18},{17,... | collective-permute-start | bytes 393224 | tf_op jit(solution)/shard_map/ppermute | solution.py:366
  14.3 1.3 %collective-permute-start.4 = (bf16[512,128]{1,0:T(8,128)(2,1)S(1)}, bf16[512,128]{1,0:T(8,128)(2,1)S(1)}, u32[]{:S(2)}, u32[]{:S(2)}) collective-permute-start(bf16[512,128]{1,0:T(8,128)(2,1)S(1)} %collective-permute-done.2), channel_id=1, source_target_pairs={{0,2},{1,3},{6,4},{7,5},{8,10},{9,11},{14,12},{15,13},{16,18},{17,... | collective-permute-start | bytes 393224 | tf_op jit(solution)/shard_map/ppermute | solution.py:366
  16.6 5.3 %shard_map.87 = f32[4,28,16,128]{3,2,1,0:T(8,128)} custom-call(s32[8]{0:T(128)S(1)} %pad_add_fusion.1.order_ref, s32[24,27]{1,0:T(8,128)S(1)} %fusion.18.picks, bf16[3072,128]{1,0:T(8,128)(2,1)S(1)} %bitcast.106, bf16[24,128,128]{2,1,0:T(8,128)(2,1)S(1)} %get-tuple-element.35.rest_0_, bf16[4,128,128]{2,1,0:T(8,128)(2,1)S(1)} %bitcast.108, ...), custom_call_target="tpu_custom_call" | custom-call | flops 10000000 | bytes 65536 | tf_op jit(solution)/shard_map/pallas_call | solution.py:170
  22.3 4.3 %shard_map.88 = f32[4,28,16,128]{3,2,1,0:T(8,128)S(1)} custom-call(s32[8]{0:T(128)S(1)} %pad_add_fusion.order_ref, s32[24,27]{1,0:T(8,128)S(1)} %fusion.18.picks, bf16[3072,128]{1,0:T(8,128)(2,1)S(1)} %bitcast.107, bf16[24,128,128]{2,1,0:T(8,128)(2,1)S(1)} %get-tuple-element.35.rest_0_, bf16[4,128,128]{2,1,0:T(8,128)(2,1)S(1)} %bitcast.109, ...), custom_call_target="tpu_custom_call" | custom-call | flops 10000000 | bytes 65536 | tf_op jit(solution)/shard_map/pallas_call | solution.py:170
  26.7 1.4 %add.139 = f32[4,28,16,128]{3,2,1,0:T(8,128)S(1)} add(f32[4,28,16,128]{3,2,1,0:T(8,128)S(1)} %shard_map.88, f32[4,28,16,128]{3,2,1,0:T(8,128)} %collective-permute-done.5) | non-fusion elementwise | flops 229376 | bytes 2752512 | tf_op jit(solution)/shard_map/add | solution.py:435
  29.4 10.0 %shard_map.89 = (f32[24,128,128]{2,1,0:T(8,128)S(1)}, f32[12,128,128]{2,1,0:T(8,128)S(1)}, f32[4,128,128]{2,1,0:T(8,128)S(1)}, f32[4,128,128]{2,1,0:T(8,128)S(1)}) custom-call(s32[24,27]{1,0:T(8,128)S(1)} %fusion.18.picks, bf16[24,128,128]{2,1,0:T(8,128)(2,1)S(1)} %get-tuple-element.42.grad_ref, bf16[3456,128]{1,0:T(8,128)(2,1)S(1)} %bitcast.103), custom_call_target="tpu_custom_call" | custom-call | flops 10000000 | bytes 65536 | tf_op jit(solution)/shard_map/pallas_call | solution.py:94
  39.7 1.5 %collective-permute-start.7 = (f16[1,28,16,128]{3,2,1,0:T(8,128)(2,1)S(1)}, f16[1,28,16,128]{3,2,1,0:T(8,128)(2,1)S(1)}, u32[]{:S(2)}, u32[]{:S(2)}) collective-permute-start(f16[1,28,16,128]{3,2,1,0:T(8,128)(2,1)S(1)} %get-tuple-element.45), channel_id=1, source_target_pairs={{0,1},{1,0},{2,6},{3,7},{4,5},{5,4},{6,2},{7,3},{8,9},{9,8},{10,14... | collective-permute-start | bytes 344072 | tf_op jit(solution)/shard_map/ppermute | solution.py:366
  41.2 3.9 %shard_map.90.rest_0_ = bf16[1536,128]{1,0:T(8,128)(2,1)S(1)} custom-call(s32[24,27]{1,0:T(8,128)S(1)} %fusion.18.picks, bf16[3456,128]{1,0:T(8,128)(2,1)S(1)} %bitcast.104, bf16[24,128,128]{2,1,0:T(8,128)(2,1)S(1)} %bitcast.101, bf16[4,128,128]{2,1,0:T(8,128)(2,1)S(1)} %bitcast.110, bf16[4,128,128]{2,1,0:T(8,128)(2,1)S(1)} %bitcast.114, ...), custom_call_target="tpu_custom_call" | custom-call | flops 10000000 | bytes 65536 | tf_op jit(solution)/shard_map/pallas_call | solution.py:220
  45.4 2.7 %collective-permute-start.9 = (f16[1,28,16,128]{3,2,1,0:T(8,128)(2,1)S(1)}, f16[1,28,16,128]{3,2,1,0:T(8,128)(2,1)S(1)}, u32[]{:S(2)}, u32[]{:S(2)}) collective-permute-start(f16[1,28,16,128]{3,2,1,0:T(8,128)(2,1)S(1)} %select_convert_fusion.2), channel_id=1, source_target_pairs={{0,16},{1,17},{2,18},{3,19},{4,20},{5,21},{6,22},{7,23},{8,24},{9,... | collective-permute-start | bytes 344072 | tf_op jit(solution)/shard_map/ppermute | solution.py:366
  50.3 4.1 %collective-permute-done.9 = f16[1,28,16,128]{3,2,1,0:T(8,128)(2,1)S(1)} collective-permute-done((f16[1,28,16,128]{3,2,1,0:T(8,128)(2,1)S(1)}, f16[1,28,16,128]{3,2,1,0:T(8,128)(2,1)S(1)}, u32[]{:S(2)}, u32[]{:S(2)}) %collective-permute-start.9) | collective-permute-done | bytes 114720 | tf_op jit(solution)/shard_map/ppermute | solution.py:366
  54.7 2.8 %collective-permute-done.11 = f32[4,128,128]{2,1,0:T(8,128)S(1)} collective-permute-done((f32[4,128,128]{2,1,0:T(8,128)S(1)}, f32[4,128,128]{2,1,0:T(8,128)S(1)}, u32[]{:S(2)}, u32[]{:S(2)}) %collective-permute-start.11) | collective-permute-done | bytes 262176 | tf_op jit(solution)/shard_map/ppermute | solution.py:366
  57.4 2.8 %collective-permute-done.10.rest_1_ = f32[4,128,128]{2,1,0:T(8,128)S(1)} collective-permute-done((f32[4,128,128]{2,1,0:T(8,128)S(1)}, f32[4,128,128]{2,1,0:T(8,128)S(1)}, u32[]{:S(2)}, u32[]{:S(2)}) %collective-permute-start.10) | collective-permute-done | bytes 262176 | tf_op jit(solution)/shard_map/ppermute | solution.py:366
  60.2 1.6 %collective-permute-start.12 = (f16[1,28,16,128]{3,2,1,0:T(8,128)(2,1)S(1)}, f16[1,28,16,128]{3,2,1,0:T(8,128)(2,1)S(1)}, u32[]{:S(2)}, u32[]{:S(2)}) collective-permute-start(f16[1,28,16,128]{3,2,1,0:T(8,128)(2,1)S(1)} %select_convert_fusion.1), channel_id=1, source_target_pairs={{0,8},{1,9},{2,10},{3,11},{4,12},{5,13},{6,14},{7,15},{8,0},{9,1},... | collective-permute-start | bytes 344072 | tf_op jit(solution)/shard_map/ppermute | solution.py:366
  61.8 1.3 %collective-permute-start.14 = (f32[4,128,128]{2,1,0:T(8,128)S(1)}, f32[4,128,128]{2,1,0:T(8,128)S(1)}, u32[]{:S(2)}, u32[]{:S(2)}) collective-permute-start(f32[4,128,128]{2,1,0:T(8,128)S(1)} %collective-permute-done.11), channel_id=1, source_target_pairs={{0,2},{1,3},{6,4},{7,5},{8,10},{9,11},{14,12},{15,13},{16,18},{17,... | collective-permute-start | bytes 786440 | tf_op jit(solution)/shard_map/ppermute | solution.py:366
  63.2 4.8 %shard_map.91 = bf16[3072,128]{1,0:T(8,128)(2,1)} custom-call(s32[24,27]{1,0:T(8,128)S(1)} %fusion.18.picks, bf16[3456,128]{1,0:T(8,128)(2,1)S(1)} %bitcast.105, bf16[1536,128]{1,0:T(8,128)(2,1)S(1)} %shard_map.90.rest_0_, bf16[24,128,128]{2,1,0:T(8,128)(2,1)S(1)} %bitcast.102, bf16[4,128,128]{2,1,0:T(8,128)(2,1)S(1)} %bitcast.111, ...), custom_call_target="tpu_custom_call" | custom-call | flops 10000000 | bytes 65536 | tf_op jit(solution)/shard_map/pallas_call | solution.py:220
  69.2 3.9 %collective-permute-done.13 = f16[1,28,16,128]{3,2,1,0:T(8,128)(2,1)S(1)} collective-permute-done((f16[1,28,16,128]{3,2,1,0:T(8,128)(2,1)S(1)}, f16[1,28,16,128]{3,2,1,0:T(8,128)(2,1)S(1)}, u32[]{:S(2)}, u32[]{:S(2)}) %collective-permute-start.13) | collective-permute-done | bytes 114720 | tf_op jit(solution)/shard_map/ppermute | solution.py:366
  73.2 1.6 %shard_map.92 = bf16[24,128,128]{2,1,0:T(8,128)(2,1)} custom-call(s32[4]{0:T(128)S(1)} %bitcast.132, s32[1]{0:T(128)} %bitcast.98.count_ref, f32[24,128,128]{2,1,0:T(8,128)S(1)} %get-tuple-element.58.own_ref, f32[4,128,128]{2,1,0:T(8,128)S(1)} %select_add_fusion.1.rest_0_, f32[4,128,128]{2,1,0:T(8,128)S(1)} %collective-permute-done.10.rest_1_, ...), custom_call_target="tpu_custom_call" | custom-call | flops 10000000 | bytes 65536 | tf_op jit(solution)/shard_map/pallas_call | solution.py:247
  75.0 5.9 %collective-permute-done.15 = f16[2,28,16,128]{3,2,1,0:T(8,128)(2,1)S(1)} collective-permute-done((f16[2,28,16,128]{3,2,1,0:T(8,128)(2,1)S(1)}, f16[2,28,16,128]{3,2,1,0:T(8,128)(2,1)S(1)}, u32[]{:S(2)}, u32[]{:S(2)}) %collective-permute-start.15) | collective-permute-done | bytes 229408 | tf_op jit(solution)/shard_map/ppermute | solution.py:366
  81.0 1.4 %collective-permute-done.17 = f16[2,28,16,128]{3,2,1,0:T(8,128)(2,1)S(1)} collective-permute-done((f16[2,28,16,128]{3,2,1,0:T(8,128)(2,1)S(1)}, f16[2,28,16,128]{3,2,1,0:T(8,128)(2,1)S(1)}, u32[]{:S(2)}, u32[]{:S(2)}) %collective-permute-start.17) | collective-permute-done | bytes 229408 | tf_op jit(solution)/shard_map/ppermute | solution.py:366
  82.6 1.8 %shard_map.93 = f32[27,128,128]{2,1,0:T(8,128)} custom-call(s32[8]{0:T(128)S(1)} %pad_add_fusion.2.order_ref, f32[2,28,16,128]{3,2,1,0:T(8,128)S(1)} %get-tuple-element.100.rest_0_, f32[2,28,16,128]{3,2,1,0:T(8,128)S(1)} %get-tuple-element.101.rest_1_, f32[2,28,16,128]{3,2,1,0:T(8,128)S(1)} %get-tuple-element.102.rest_2_, ...), custom_call_target="tpu_custom_call" | custom-call | tf_op jit(solution)/shard_map/pallas_call | solution.py:278
  (81 shorter events, 10.8 us)
Async XLA Ops:
  0.6 8.1 %copy-start = (bf16[1,1,1,3072,128]{4,3,2,1,0:T(8,128)(2,1)S(1)}, bf16[1,1,1,3072,128]{4,3,2,1,0:T(8,128)(2,1)}, u32[]{:S(2)}) copy-start(bf16[1,1,1,3072,128]{4,3,2,1,0:T(8,128)(2,1)} %param.6) | copy-start | bytes 2359300
  1.4 0.7 copy-start.3
  3.4 3.1 %collective-permute-start.1 = (bf16[512,128]{1,0:T(8,128)(2,1)S(1)}, bf16[512,128]{1,0:T(8,128)(2,1)S(1)}, u32[]{:S(2)}, u32[]{:S(2)}) collective-permute-start(bf16[512,128]{1,0:T(8,128)(2,1)S(1)} %bitcast.129), channel_id=1, source_target_pairs={{0,2},{1,3},{2,0},{3,1},{4,6},{5,7},{6,4},{7,5},{8,10},{9,11},{10,... | collective-permute-start | bytes 393224 | tf_op jit(solution)/shard_map/ppermute | solution.py:366
  3.9 6.2 %collective-permute-start = (bf16[512,128]{1,0:T(8,128)(2,1)S(1)}, bf16[512,128]{1,0:T(8,128)(2,1)S(1)}, u32[]{:S(2)}, u32[]{:S(2)}) collective-permute-start(bf16[512,128]{1,0:T(8,128)(2,1)S(1)} %bitcast.130), channel_id=1, source_target_pairs={{0,1},{1,0},{2,4},{3,5},{4,2},{5,3},{6,7},{7,6},{8,9},{9,8},{10,12... | collective-permute-start | bytes 393224 | tf_op jit(solution)/shard_map/ppermute | solution.py:366
  6.6 6.4 %collective-permute-start.2 = (bf16[512,128]{1,0:T(8,128)(2,1)S(1)}, bf16[512,128]{1,0:T(8,128)(2,1)S(1)}, u32[]{:S(2)}, u32[]{:S(2)}) collective-permute-start(bf16[512,128]{1,0:T(8,128)(2,1)S(1)} %broadcast_select_fusion), channel_id=1, source_target_pairs={{0,1},{1,0},{2,5},{3,4},{4,3},{5,2},{6,7},{7,6},{8,9},{9,8},{10,13... | collective-permute-start | bytes 393224 | tf_op jit(solution)/shard_map/ppermute | solution.py:366
  8.7 1.1 %copy-start.2 = (bf16[1,1,1,3072,128]{4,3,2,1,0:T(8,128)(2,1)S(1)}, bf16[1,1,1,3072,128]{4,3,2,1,0:T(8,128)(2,1)}, u32[]{:S(2)}) copy-start(bf16[1,1,1,3072,128]{4,3,2,1,0:T(8,128)(2,1)} %param.7) | copy-start | bytes 2359300
  13.0 2.7 %collective-permute-start.3 = (bf16[512,128]{1,0:T(8,128)(2,1)S(1)}, bf16[512,128]{1,0:T(8,128)(2,1)S(1)}, u32[]{:S(2)}, u32[]{:S(2)}) collective-permute-start(bf16[512,128]{1,0:T(8,128)(2,1)S(1)} %collective-permute-done), channel_id=1, source_target_pairs={{0,2},{1,3},{6,4},{7,5},{8,10},{9,11},{14,12},{15,13},{16,18},{17,... | collective-permute-start | bytes 393224 | tf_op jit(solution)/shard_map/ppermute | solution.py:366
  14.3 2.3 %collective-permute-start.4 = (bf16[512,128]{1,0:T(8,128)(2,1)S(1)}, bf16[512,128]{1,0:T(8,128)(2,1)S(1)}, u32[]{:S(2)}, u32[]{:S(2)}) collective-permute-start(bf16[512,128]{1,0:T(8,128)(2,1)S(1)} %collective-permute-done.2), channel_id=1, source_target_pairs={{0,2},{1,3},{6,4},{7,5},{8,10},{9,11},{14,12},{15,13},{16,18},{17,... | collective-permute-start | bytes 393224 | tf_op jit(solution)/shard_map/ppermute | solution.py:366
  21.8 4.8 %collective-permute-start.5 = (f32[4,28,16,128]{3,2,1,0:T(8,128)}, f32[4,28,16,128]{3,2,1,0:T(8,128)}, u32[]{:S(2)}, u32[]{:S(2)}) collective-permute-start(f32[4,28,16,128]{3,2,1,0:T(8,128)} %shard_map.87), channel_id=1, source_target_pairs={{0,2},{1,3},{2,0},{3,1},{4,6},{5,7},{6,4},{7,5},{8,10},{9,11},{10,... | collective-permute-start | bytes 2752520 | tf_op jit(solution)/shard_map/ppermute | solution.py:366
  26.7 2.7 %copy-start.1 = (bf16[27,128,128]{2,1,0:T(8,128)(2,1)S(1)}, bf16[27,128,128]{2,1,0:T(8,128)(2,1)}, u32[]{:S(2)}) copy-start(bf16[27,128,128]{2,1,0:T(8,128)(2,1)} %param.8) | copy-start | bytes 2654212
  28.2 11.2 %collective-permute-start.6 = (f16[2,28,16,128]{3,2,1,0:T(8,128)(2,1)S(1)}, f16[2,28,16,128]{3,2,1,0:T(8,128)(2,1)S(1)}, u32[]{:S(2)}, u32[]{:S(2)}) collective-permute-start(f16[2,28,16,128]{3,2,1,0:T(8,128)(2,1)S(1)} %get-tuple-element.41), channel_id=1, source_target_pairs={{0,4},{1,5},{2,3},{3,2},{4,0},{5,1},{6,7},{7,6},{8,12},{9,13},{10,... | collective-permute-start | bytes 688136 | tf_op jit(solution)/shard_map/ppermute | solution.py:366
  39.7 5.4 %collective-permute-start.7 = (f16[1,28,16,128]{3,2,1,0:T(8,128)(2,1)S(1)}, f16[1,28,16,128]{3,2,1,0:T(8,128)(2,1)S(1)}, u32[]{:S(2)}, u32[]{:S(2)}) collective-permute-start(f16[1,28,16,128]{3,2,1,0:T(8,128)(2,1)S(1)} %get-tuple-element.45), channel_id=1, source_target_pairs={{0,1},{1,0},{2,6},{3,7},{4,5},{5,4},{6,2},{7,3},{8,9},{9,8},{10,14... | collective-permute-start | bytes 344072 | tf_op jit(solution)/shard_map/ppermute | solution.py:366
  41.2 4.2 %collective-permute-start.8 = (f32[12,128,128]{2,1,0:T(8,128)S(1)}, f32[12,128,128]{2,1,0:T(8,128)S(1)}, u32[]{:S(2)}, u32[]{:S(2)}) collective-permute-start(f32[12,128,128]{2,1,0:T(8,128)S(1)} %get-tuple-element.46), channel_id=1, source_target_pairs={{0,2},{1,3},{2,0},{3,1},{4,6},{5,7},{6,4},{7,5},{8,10},{9,11},{10,... | collective-permute-start | bytes 2359304 | tf_op jit(solution)/shard_map/ppermute | solution.py:366
  45.4 9.0 %collective-permute-start.9 = (f16[1,28,16,128]{3,2,1,0:T(8,128)(2,1)S(1)}, f16[1,28,16,128]{3,2,1,0:T(8,128)(2,1)S(1)}, u32[]{:S(2)}, u32[]{:S(2)}) collective-permute-start(f16[1,28,16,128]{3,2,1,0:T(8,128)(2,1)S(1)} %select_convert_fusion.2), channel_id=1, source_target_pairs={{0,16},{1,17},{2,18},{3,19},{4,20},{5,21},{6,22},{7,23},{8,24},{9,... | collective-permute-start | bytes 344072 | tf_op jit(solution)/shard_map/ppermute | solution.py:366
  48.2 9.2 %collective-permute-start.11 = (f32[4,128,128]{2,1,0:T(8,128)S(1)}, f32[4,128,128]{2,1,0:T(8,128)S(1)}, u32[]{:S(2)}, u32[]{:S(2)}) collective-permute-start(f32[4,128,128]{2,1,0:T(8,128)S(1)} %get-tuple-element.67), channel_id=1, source_target_pairs={{0,1},{1,0},{2,5},{3,4},{4,3},{5,2},{6,7},{7,6},{8,9},{9,8},{10,13... | collective-permute-start | bytes 786440 | tf_op jit(solution)/shard_map/ppermute | solution.py:366
  49.1 11.2 %collective-permute-start.10 = (f32[4,128,128]{2,1,0:T(8,128)S(1)}, f32[4,128,128]{2,1,0:T(8,128)S(1)}, u32[]{:S(2)}, u32[]{:S(2)}) collective-permute-start(f32[4,128,128]{2,1,0:T(8,128)S(1)} %get-tuple-element.68), channel_id=1, source_target_pairs={{0,1},{1,0},{2,4},{3,5},{4,2},{5,3},{6,7},{7,6},{8,9},{9,8},{10,12... | collective-permute-start | bytes 786440 | tf_op jit(solution)/shard_map/ppermute | solution.py:366
  60.2 7.8 %collective-permute-start.12 = (f16[1,28,16,128]{3,2,1,0:T(8,128)(2,1)S(1)}, f16[1,28,16,128]{3,2,1,0:T(8,128)(2,1)S(1)}, u32[]{:S(2)}, u32[]{:S(2)}) collective-permute-start(f16[1,28,16,128]{3,2,1,0:T(8,128)(2,1)S(1)} %select_convert_fusion.1), channel_id=1, source_target_pairs={{0,8},{1,9},{2,10},{3,11},{4,12},{5,13},{6,14},{7,15},{8,0},{9,1},... | collective-permute-start | bytes 344072 | tf_op jit(solution)/shard_map/ppermute | solution.py:366
  61.8 11.4 %collective-permute-start.14 = (f32[4,128,128]{2,1,0:T(8,128)S(1)}, f32[4,128,128]{2,1,0:T(8,128)S(1)}, u32[]{:S(2)}, u32[]{:S(2)}) collective-permute-start(f32[4,128,128]{2,1,0:T(8,128)S(1)} %collective-permute-done.11), channel_id=1, source_target_pairs={{0,2},{1,3},{6,4},{7,5},{8,10},{9,11},{14,12},{15,13},{16,18},{17,... | collective-permute-start | bytes 786440 | tf_op jit(solution)/shard_map/ppermute | solution.py:366
  68.0 5.2 %copy-start.4 = (s32[1,1,1,4]{3,2,1,0:T(1,128)S(1)}, s32[1,1,1,4]{3,2,1,0:T(1,128)}, u32[]{:S(2)}) copy-start(s32[1,1,1,4]{3,2,1,0:T(1,128)} %param.10) | copy-start | bytes 52
  68.3 4.9 %collective-permute-start.13 = (f16[1,28,16,128]{3,2,1,0:T(8,128)(2,1)S(1)}, f16[1,28,16,128]{3,2,1,0:T(8,128)(2,1)S(1)}, u32[]{:S(2)}, u32[]{:S(2)}) collective-permute-start(f16[1,28,16,128]{3,2,1,0:T(8,128)(2,1)S(1)} %select_convert_fusion), channel_id=1, source_target_pairs={{0,1},{1,0},{2,6},{3,7},{4,5},{5,4},{6,2},{7,3},{8,9},{9,8},{10,14... | collective-permute-start | bytes 344072 | tf_op jit(solution)/shard_map/ppermute | solution.py:366
  74.8 6.0 %collective-permute-start.15 = (f16[2,28,16,128]{3,2,1,0:T(8,128)(2,1)S(1)}, f16[2,28,16,128]{3,2,1,0:T(8,128)(2,1)S(1)}, u32[]{:S(2)}, u32[]{:S(2)}) collective-permute-start(f16[2,28,16,128]{3,2,1,0:T(8,128)(2,1)S(1)} %pad_maximum_fusion), channel_id=1, source_target_pairs={{0,4},{1,5},{2,3},{3,2},{4,0},{5,1},{6,7},{7,6},{8,12},{9,13},{10,... | collective-permute-start | bytes 688136 | tf_op jit(solution)/shard_map/ppermute | solution.py:366
  74.9 6.0 %collective-permute-start.16 = (f16[2,28,16,128]{3,2,1,0:T(8,128)(2,1)S(1)}, f16[2,28,16,128]{3,2,1,0:T(8,128)(2,1)S(1)}, u32[]{:S(2)}, u32[]{:S(2)}) collective-permute-start(f16[2,28,16,128]{3,2,1,0:T(8,128)(2,1)S(1)} %pad_maximum_fusion), channel_id=1, source_target_pairs={{0,2},{1,3},{2,0},{3,1},{4,6},{5,7},{6,4},{7,5},{8,10},{9,11},{10,... | collective-permute-start | bytes 688136 | tf_op jit(solution)/shard_map/ppermute | solution.py:366
  80.8 1.5 %collective-permute-start.17 = (f16[2,28,16,128]{3,2,1,0:T(8,128)(2,1)S(1)}, f16[2,28,16,128]{3,2,1,0:T(8,128)(2,1)S(1)}, u32[]{:S(2)}, u32[]{:S(2)}) collective-permute-start(f16[2,28,16,128]{3,2,1,0:T(8,128)(2,1)S(1)} %collective-permute-done.15), channel_id=1, source_target_pairs={{0,2},{1,3},{2,0},{3,1},{4,6},{5,7},{6,4},{7,5},{8,10},{9,11},{10,... | collective-permute-start | bytes 688136 | tf_op jit(solution)/shard_map/ppermute | solution.py:366

commit v3 on v2

--- a/solution.py
+++ b/solution.py
@@ -22,7 +22,7 @@
 
 
 def cost(flops):
-    return pl.CostEstimate(flops=flops, bytes_accessed=2**16, transcendentals=0)
+    return pl.CostEstimate(flops=flops, bytes_accessed=4 * 2**20, transcendentals=0)
 
 
 def outgoing_kernel(sent_ref, count_ref, x_ref, out_ref, sems):
@@ -358,11 +358,11 @@
         def flat(z, x, c, y):
             return (z * size_x + 2 * x + c) * size_y + y
 
-        def exchange(array, to, senders=lambda z, x, c, y: True):
+        def exchange(array, to):
             places = [
                 (z, x, c, y) for z in range(4) for x in range(2) for c in range(2) for y in range(2)
             ]
-            route = [(flat(*p), flat(*to(*p))) for p in places if senders(*p)]
+            route = [(flat(*p), flat(*to(*p))) for p in places]
             return lax.ppermute(array, AXES, route)
 
         def cores(z, x, c, y):
@@ -376,15 +376,12 @@
 
         def across(z, x, c, y):
             return (z, 1 - x, 1 - c, 1 - y) if is_middle(z, x, c, y) else (z, x, c, 1 - y)
-
-        def is_end(*p):
-            return not is_middle(*p)
 
         beside = exchange(sent, cores)
         first = exchange(sent, straight)
         second = exchange(jnp.where(middle, sent, beside), across)
         first, second, turned_own = lax.optimization_barrier((first, second, turned_own))
-        passed = [exchange(first, cores, is_end), exchange(second, cores, is_end)]
+        passed = [exchange(first, cores), exchange(second, cores)]
         extended = [blocks] + [to_blocks(a) for a in [beside, first, second] + passed]
 
         core, far_x = odd, tile_x // 2
@@ -441,34 +438,34 @@
         )
         back = exchange(inner_terms, cores)
         pair = pair + decode(exchange(message, x_or_y))
-        message, part, own_terms, late_picks = lax.optimization_barrier(
-            (encode(pair[1:]), pair[:1], own_terms, picks)
-        )
+        message, part, own_terms = lax.optimization_barrier(
+            (encode(pair[1:]), pair[:1], own_terms)
+        )
+        message = encode(part + decode(exchange(message, y_or_x)))
+        message, back, late_picks = lax.optimization_barrier((message, back, picks))
+        first_back = exchange(first_terms + back[num_sent : 2 * num_sent], straight)
+        second_back = exchange(second_terms + back[2 * num_sent :], across)
         middle_block = num_blocks // 2
         upper = output_blocks(late_picks, weights, extended, (0, middle_block))
-        message = encode(part + decode(exchange(message, y_or_x)))
-        message, back, upper = lax.optimization_barrier((message, back, upper))
-        first_back = exchange(first_terms + back[num_sent : 2 * num_sent], straight)
-        second_back = exchange(second_terms + back[2 * num_sent :], across)
         part = decode(message) + decode(exchange(message, z_far))
-        message, late_picks, first_back, second_back = lax.optimization_barrier(
-            (encode(part), late_picks, first_back, second_back)
+        message, upper = lax.optimization_barrier((encode(part), upper))
+        part = decode(message) + decode(exchange(message, z_near))
+        message, first_back, second_back, late_picks = lax.optimization_barrier(
+            (encode(part), first_back, second_back, late_picks)
         )
         output = output_blocks(
             late_picks, weights, extended, (middle_block, num_blocks), (upper,)
         )
-        passed_back = exchange(second_back, cores, is_end)
-        part = decode(message) + decode(exchange(message, z_near))
+        passed_back = exchange(second_back, cores)
         returned = [
-            back[:num_sent] + jnp.where(middle, second_back, 0.0),
+            back[:num_sent] + jnp.where(middle, second_back + passed_back, 0.0),
             first_back,
-            passed_back,
         ]
-        message, output, own_terms = lax.optimization_barrier((encode(part), output, own_terms))
+        pair = jnp.concatenate([message, exchange(message, y_or_x)])
+        pair, output, own_terms = lax.optimization_barrier((pair, output, own_terms))
         input_grad = input_grad_blocks(sent_ids, count, own_terms, returned)
-        pair = jnp.concatenate([message, exchange(message, y_or_x)])
-        pair, input_grad = lax.optimization_barrier((pair, input_grad))
         rest = exchange(pair, x_or_y)
+        rest, input_grad = lax.optimization_barrier((rest, input_grad))
         messages = [pair, rest, exchange(pair, cores), exchange(rest, cores)]
         weight_grad = assemble(order, [decode(m) for m in messages])
 

time: 84.8 us -> 73.5 us (0.87)
  waiting for transfers between devices: 24.6 us -> 15.6 us
  starting transfers between devices: 18.6 us -> 16.3 us
    ppermute x18, waiting for transfers between devices: 24.6 us -> 15.6 us  [exchange(): return lax.ppermute(array, AXES, route)]
    ppermute x18, starting transfers between devices: 18.6 us -> 16.3 us  [exchange(): return lax.ppermute(array, AXES, route)]
  transfers between devices with their start and end apart: 18 -> 18, of which waited for: 8 -> 7; matrix products, arithmetic and copies ran while one was open for 3% -> 3% of each run, Pallas kernels for 28% -> 34%
where the time goes in v3:
time: 73.5 us; the launch traced here: 73.1 us
  Pallas kernels  33.4 us (45%)
  starting transfers between devices  16.3 us (22%)
  waiting for transfers between devices  15.6 us (21%)
  other arithmetic  4.28 us (6%)
  local copies, waits for them, and re-layouts  1.79 us (2%)
  between operations  1.78 us (2%)
    ppermute x18, starting transfers between devices, exchange(): return lax.ppermute(array, AXES, route)  16.3 us
    ppermute x18, waiting for transfers between devices, exchange(): return lax.ppermute(array, AXES, route)  15.6 us
    pallas_call x1, Pallas kernels, input_terms(): pl.pallas_call(functools.partial(input_terms_kernel, halo_spans), out_sha...  10 us
    pallas_call x2, Pallas kernels, weight_terms(): pl.pallas_call(functools.partial(weight_terms_kernel, scale, group), out_...  9.62 us
    pallas_call x2, Pallas kernels, output_blocks(): pl.pallas_call(functools.partial(output_kernel, group, span, len(done)),...  8.75 us
    pallas_call x1, Pallas kernels, assemble(): pl.pallas_call(assemble_kernel, out_shape=jax.ShapeDtypeStruct((slots - 1...  1.81 us
    unnamed x10, local copies, waits for them, and re-layouts  1.79 us
    pallas_call x1, Pallas kernels, input_grad_blocks(): pl.pallas_call(input_grad_kernel, out_shape=jax.ShapeDtypeStruct(own.shap...  1.55 us
  transfers between devices with their start and end apart: 18, of which 7 were waited for; matrix products, arithmetic and copies ran while one was open for 3% of the time, Pallas kernels for 34%

profile of v3, /device:TPU:0, one launch (start us, length us, event | category | flops | bytes accessed | tf_op | source)
XLA Modules:
  0.0 73.1 jit_solution(80692375068421674)
XLA Ops:
  2.0 1.4 %shard_map.86 = bf16[4,128,128]{2,1,0:T(8,128)(2,1)S(1)} custom-call(s32[4]{0:T(128)S(1)} %bitcast.131, s32[1]{0:T(128)} %bitcast.97.count_ref, bf16[24,128,128]{2,1,0:T(8,128)(2,1)} %bitcast.99), custom_call_target="tpu_custom_call" | custom-call | bytes 262144 | tf_op jit(solution)/shard_map/pallas_call | solution.py:47
  3.9 2.6 %collective-permute-start = (bf16[512,128]{1,0:T(8,128)(2,1)S(1)}, bf16[512,128]{1,0:T(8,128)(2,1)S(1)}, u32[]{:S(2)}, u32[]{:S(2)}) collective-permute-start(bf16[512,128]{1,0:T(8,128)(2,1)S(1)} %bitcast.130), channel_id=1, source_target_pairs={{0,1},{1,0},{2,4},{3,5},{4,2},{5,3},{6,7},{7,6},{8,9},{9,8},{10,12... | collective-permute-start | bytes 393224 | tf_op jit(solution)/shard_map/ppermute | solution.py:366
  6.6 1.3 %collective-permute-start.2 = (bf16[512,128]{1,0:T(8,128)(2,1)S(1)}, bf16[512,128]{1,0:T(8,128)(2,1)S(1)}, u32[]{:S(2)}, u32[]{:S(2)}) collective-permute-start(bf16[512,128]{1,0:T(8,128)(2,1)S(1)} %broadcast_select_fusion), channel_id=1, source_target_pairs={{0,1},{1,0},{2,5},{3,4},{4,3},{5,2},{6,7},{7,6},{8,9},{9,8},{10,13... | collective-permute-start | bytes 393224 | tf_op jit(solution)/shard_map/ppermute | solution.py:366
  7.9 0.8 %fusion.18.picks = s32[24,27]{1,0:T(8,128)S(1)} fusion(s32[1,1,1,27,24]{3,4,2,1,0:T(8,128)} %param.9, s32[]{:T(128)S(6)} %select_n.180, s32[]{:T(128)S(6)} %sub.64, s32[]{:T(128)S(6)} %select_n.179, s32[]{:T(128)S(6)} %axis_index.25, s32[]{:T(128)S(6)} %axis_index.23, s32[]{:T(128)} %bitcast.95, pred[24]{0:T(512)(128)(4,1)S(1)} %iota_compare_fusion), kind=kLoop, calls=%fused_computation.59 | loop fusion | flops 43416 | bytes 5232 | tf_op jit(solution)/shard_map/jit(_where)/select_n | solution.py:351
  8.7 1.1 %copy-done.2 = bf16[1,1,1,3072,128]{4,3,2,1,0:T(8,128)(2,1)S(1)} copy-done((bf16[1,1,1,3072,128]{4,3,2,1,0:T(8,128)(2,1)S(1)}, bf16[1,1,1,3072,128]{4,3,2,1,0:T(8,128)(2,1)}, u32[]{:S(2)}) %copy-start.2) | copy-done | bytes 786456
  10.1 2.9 %collective-permute-done.2 = bf16[512,128]{1,0:T(8,128)(2,1)S(1)} collective-permute-done((bf16[512,128]{1,0:T(8,128)(2,1)S(1)}, bf16[512,128]{1,0:T(8,128)(2,1)S(1)}, u32[]{:S(2)}, u32[]{:S(2)}) %collective-permute-start.2) | collective-permute-done | bytes 131104 | tf_op jit(solution)/shard_map/ppermute | solution.py:366
  14.5 5.3 %shard_map.87 = f32[4,28,16,128]{3,2,1,0:T(8,128)} custom-call(s32[8]{0:T(128)S(1)} %pad_add_fusion.1.order_ref, s32[24,27]{1,0:T(8,128)S(1)} %fusion.18.picks, bf16[3072,128]{1,0:T(8,128)(2,1)S(1)} %bitcast.106, bf16[24,128,128]{2,1,0:T(8,128)(2,1)S(1)} %get-tuple-element.36.rest_0_, bf16[4,128,128]{2,1,0:T(8,128)(2,1)S(1)} %bitcast.108, ...), custom_call_target="tpu_custom_call" | custom-call | flops 10000000 | bytes 4194304 | tf_op jit(solution)/shard_map/pallas_call | solution.py:170
  20.2 4.3 %shard_map.88 = f32[4,28,16,128]{3,2,1,0:T(8,128)S(1)} custom-call(s32[8]{0:T(128)S(1)} %pad_add_fusion.order_ref, s32[24,27]{1,0:T(8,128)S(1)} %fusion.18.picks, bf16[3072,128]{1,0:T(8,128)(2,1)S(1)} %bitcast.107, bf16[24,128,128]{2,1,0:T(8,128)(2,1)S(1)} %get-tuple-element.36.rest_0_, bf16[4,128,128]{2,1,0:T(8,128)(2,1)S(1)} %bitcast.109, ...), custom_call_target="tpu_custom_call" | custom-call | flops 10000000 | bytes 4194304 | tf_op jit(solution)/shard_map/pallas_call | solution.py:170
  24.6 1.4 %add.142 = f32[4,28,16,128]{3,2,1,0:T(8,128)S(1)} add(f32[4,28,16,128]{3,2,1,0:T(8,128)S(1)} %shard_map.88, f32[4,28,16,128]{3,2,1,0:T(8,128)} %collective-permute-done.5) | non-fusion elementwise | flops 229376 | bytes 2752512 | tf_op jit(solution)/shard_map/add | solution.py:432
  26.5 10.0 %shard_map.89 = (f32[24,128,128]{2,1,0:T(8,128)S(1)}, f32[12,128,128]{2,1,0:T(8,128)S(1)}, f32[4,128,128]{2,1,0:T(8,128)S(1)}, f32[4,128,128]{2,1,0:T(8,128)S(1)}) custom-call(s32[24,27]{1,0:T(8,128)S(1)} %fusion.18.picks, bf16[24,128,128]{2,1,0:T(8,128)(2,1)S(1)} %get-tuple-element.43.grad_ref, bf16[3456,128]{1,0:T(8,128)(2,1)S(1)} %bitcast.103), custom_call_target="tpu_custom_call" | custom-call | flops 10000000 | bytes 4194304 | tf_op jit(solution)/shard_map/pallas_call | solution.py:94
  36.9 1.5 %collective-permute-start.7 = (f16[1,28,16,128]{3,2,1,0:T(8,128)(2,1)S(1)}, f16[1,28,16,128]{3,2,1,0:T(8,128)(2,1)S(1)}, u32[]{:S(2)}, u32[]{:S(2)}) collective-permute-start(f16[1,28,16,128]{3,2,1,0:T(8,128)(2,1)S(1)} %get-tuple-element.46), channel_id=1, source_target_pairs={{0,1},{1,0},{2,6},{3,7},{4,5},{5,4},{6,2},{7,3},{8,9},{9,8},{10,14... | collective-permute-start | bytes 344072 | tf_op jit(solution)/shard_map/ppermute | solution.py:366
  38.4 3.4 %collective-permute-done.7 = f16[1,28,16,128]{3,2,1,0:T(8,128)(2,1)S(1)} collective-permute-done((f16[1,28,16,128]{3,2,1,0:T(8,128)(2,1)S(1)}, f16[1,28,16,128]{3,2,1,0:T(8,128)(2,1)S(1)}, u32[]{:S(2)}, u32[]{:S(2)}) %collective-permute-start.7) | collective-permute-done | bytes 114720 | tf_op jit(solution)/shard_map/ppermute | solution.py:366
  42.0 2.6 %collective-permute-start.9 = (f16[1,28,16,128]{3,2,1,0:T(8,128)(2,1)S(1)}, f16[1,28,16,128]{3,2,1,0:T(8,128)(2,1)S(1)}, u32[]{:S(2)}, u32[]{:S(2)}) collective-permute-start(f16[1,28,16,128]{3,2,1,0:T(8,128)(2,1)S(1)} %select_convert_fusion.2), channel_id=1, source_target_pairs={{0,16},{1,17},{2,18},{3,19},{4,20},{5,21},{6,22},{7,23},{8,24},{9,... | collective-permute-start | bytes 344072 | tf_op jit(solution)/shard_map/ppermute | solution.py:366
  44.7 1.6 %collective-permute-start.12 = (f32[4,128,128]{2,1,0:T(8,128)S(1)}, f32[4,128,128]{2,1,0:T(8,128)S(1)}, u32[]{:S(2)}, u32[]{:S(2)}) collective-permute-start(f32[4,128,128]{2,1,0:T(8,128)S(1)} %get-tuple-element.69), channel_id=1, source_target_pairs={{0,1},{1,0},{2,5},{3,4},{4,3},{5,2},{6,7},{7,6},{8,9},{9,8},{10,13... | collective-permute-start | bytes 786440 | tf_op jit(solution)/shard_map/ppermute | solution.py:366
  46.8 3.9 %shard_map.90.rest_0_ = bf16[1536,128]{1,0:T(8,128)(2,1)S(1)} custom-call(s32[24,27]{1,0:T(8,128)S(1)} %fusion.18.picks, bf16[3456,128]{1,0:T(8,128)(2,1)S(1)} %bitcast.104, bf16[24,128,128]{2,1,0:T(8,128)(2,1)S(1)} %bitcast.101, bf16[4,128,128]{2,1,0:T(8,128)(2,1)S(1)} %bitcast.110, bf16[4,128,128]{2,1,0:T(8,128)(2,1)S(1)} %bitcast.114, ...), custom_call_target="tpu_custom_call" | custom-call | flops 10000000 | bytes 4194304 | tf_op jit(solution)/shard_map/pallas_call | solution.py:220
  51.0 1.7 %collective-permute-start.10 = (f16[1,28,16,128]{3,2,1,0:T(8,128)(2,1)S(1)}, f16[1,28,16,128]{3,2,1,0:T(8,128)(2,1)S(1)}, u32[]{:S(2)}, u32[]{:S(2)}) collective-permute-start(f16[1,28,16,128]{3,2,1,0:T(8,128)(2,1)S(1)} %select_convert_fusion.1), channel_id=1, source_target_pairs={{0,8},{1,9},{2,10},{3,11},{4,12},{5,13},{6,14},{7,15},{8,0},{9,1},... | collective-permute-start | bytes 344072 | tf_op jit(solution)/shard_map/ppermute | solution.py:366
  52.8 3.9 %collective-permute-done.10 = f16[1,28,16,128]{3,2,1,0:T(8,128)(2,1)S(1)} collective-permute-done((f16[1,28,16,128]{3,2,1,0:T(8,128)(2,1)S(1)}, f16[1,28,16,128]{3,2,1,0:T(8,128)(2,1)S(1)}, u32[]{:S(2)}, u32[]{:S(2)}) %collective-permute-start.10) | collective-permute-done | bytes 114720 | tf_op jit(solution)/shard_map/ppermute | solution.py:366
  57.0 0.9 %collective-permute-start.13 = (f16[1,28,16,128]{3,2,1,0:T(8,128)(2,1)S(1)}, f16[1,28,16,128]{3,2,1,0:T(8,128)(2,1)S(1)}, u32[]{:S(2)}, u32[]{:S(2)}) collective-permute-start(f16[1,28,16,128]{3,2,1,0:T(8,128)(2,1)S(1)} %select_convert_fusion), channel_id=1, source_target_pairs={{0,1},{1,0},{2,6},{3,7},{4,5},{5,4},{6,2},{7,3},{8,9},{9,8},{10,14... | collective-permute-start | bytes 344072 | tf_op jit(solution)/shard_map/ppermute | solution.py:366
  58.0 4.8 %shard_map.91 = bf16[3072,128]{1,0:T(8,128)(2,1)} custom-call(s32[24,27]{1,0:T(8,128)S(1)} %fusion.18.picks, bf16[3456,128]{1,0:T(8,128)(2,1)S(1)} %bitcast.105, bf16[1536,128]{1,0:T(8,128)(2,1)S(1)} %shard_map.90.rest_0_, bf16[24,128,128]{2,1,0:T(8,128)(2,1)S(1)} %bitcast.102, bf16[4,128,128]{2,1,0:T(8,128)(2,1)S(1)} %bitcast.111, ...), custom_call_target="tpu_custom_call" | custom-call | flops 10000000 | bytes 4194304 | tf_op jit(solution)/shard_map/pallas_call | solution.py:220
  63.5 1.2 %collective-permute-start.14 = (f16[2,28,16,128]{3,2,1,0:T(8,128)(2,1)S(1)}, f16[2,28,16,128]{3,2,1,0:T(8,128)(2,1)S(1)}, u32[]{:S(2)}, u32[]{:S(2)}) collective-permute-start(f16[2,28,16,128]{3,2,1,0:T(8,128)(2,1)S(1)} %pad_maximum_fusion), channel_id=1, source_target_pairs={{0,4},{1,5},{2,3},{3,2},{4,0},{5,1},{6,7},{7,6},{8,12},{9,13},{10,... | collective-permute-start | bytes 688136 | tf_op jit(solution)/shard_map/ppermute | solution.py:366
  64.9 1.6 %shard_map.92 = bf16[24,128,128]{2,1,0:T(8,128)(2,1)} custom-call(s32[4]{0:T(128)S(1)} %bitcast.132, s32[1]{0:T(128)} %bitcast.98.count_ref, f32[24,128,128]{2,1,0:T(8,128)S(1)} %get-tuple-element.60.own_ref, f32[4,128,128]{2,1,0:T(8,128)S(1)} %select_add_fusion.1.rest_0_, f32[4,128,128]{2,1,0:T(8,128)S(1)} %collective-permute-done.11.rest_1_), custom_call_target="tpu_custom_call" | custom-call | flops 10000000 | bytes 4194304 | tf_op jit(solution)/shard_map/pallas_call | solution.py:247
  66.4 3.1 %collective-permute-done.14 = f16[2,28,16,128]{3,2,1,0:T(8,128)(2,1)S(1)} collective-permute-done((f16[2,28,16,128]{3,2,1,0:T(8,128)(2,1)S(1)}, f16[2,28,16,128]{3,2,1,0:T(8,128)(2,1)S(1)}, u32[]{:S(2)}, u32[]{:S(2)}) %collective-permute-start.14) | collective-permute-done | bytes 229408 | tf_op jit(solution)/shard_map/ppermute | solution.py:366
  69.7 1.4 %collective-permute-done.17 = f16[2,28,16,128]{3,2,1,0:T(8,128)(2,1)S(1)} collective-permute-done((f16[2,28,16,128]{3,2,1,0:T(8,128)(2,1)S(1)}, f16[2,28,16,128]{3,2,1,0:T(8,128)(2,1)S(1)}, u32[]{:S(2)}, u32[]{:S(2)}) %collective-permute-start.17) | collective-permute-done | bytes 229408 | tf_op jit(solution)/shard_map/ppermute | solution.py:366
  71.3 1.8 %shard_map.93 = f32[27,128,128]{2,1,0:T(8,128)} custom-call(s32[8]{0:T(128)S(1)} %pad_add_fusion.2.order_ref, f32[2,28,16,128]{3,2,1,0:T(8,128)S(1)} %get-tuple-element.102.rest_0_, f32[2,28,16,128]{3,2,1,0:T(8,128)S(1)} %get-tuple-element.103.rest_1_, f32[2,28,16,128]{3,2,1,0:T(8,128)S(1)} %get-tuple-element.104.rest_2_, ...), custom_call_target="tpu_custom_call" | custom-call | tf_op jit(solution)/shard_map/pallas_call | solution.py:278
  (81 shorter events, 6.9 us)
Async XLA Ops:
  0.6 8.1 %copy-start = (bf16[1,1,1,3072,128]{4,3,2,1,0:T(8,128)(2,1)S(1)}, bf16[1,1,1,3072,128]{4,3,2,1,0:T(8,128)(2,1)}, u32[]{:S(2)}) copy-start(bf16[1,1,1,3072,128]{4,3,2,1,0:T(8,128)(2,1)} %param.6) | copy-start | bytes 2359300
  1.4 0.7 copy-start.3
  3.4 3.1 %collective-permute-start.1 = (bf16[512,128]{1,0:T(8,128)(2,1)S(1)}, bf16[512,128]{1,0:T(8,128)(2,1)S(1)}, u32[]{:S(2)}, u32[]{:S(2)}) collective-permute-start(bf16[512,128]{1,0:T(8,128)(2,1)S(1)} %bitcast.129), channel_id=1, source_target_pairs={{0,2},{1,3},{2,0},{3,1},{4,6},{5,7},{6,4},{7,5},{8,10},{9,11},{10,... | collective-permute-start | bytes 393224 | tf_op jit(solution)/shard_map/ppermute | solution.py:366
  3.9 6.2 %collective-permute-start = (bf16[512,128]{1,0:T(8,128)(2,1)S(1)}, bf16[512,128]{1,0:T(8,128)(2,1)S(1)}, u32[]{:S(2)}, u32[]{:S(2)}) collective-permute-start(bf16[512,128]{1,0:T(8,128)(2,1)S(1)} %bitcast.130), channel_id=1, source_target_pairs={{0,1},{1,0},{2,4},{3,5},{4,2},{5,3},{6,7},{7,6},{8,9},{9,8},{10,12... | collective-permute-start | bytes 393224 | tf_op jit(solution)/shard_map/ppermute | solution.py:366
  6.6 6.4 %collective-permute-start.2 = (bf16[512,128]{1,0:T(8,128)(2,1)S(1)}, bf16[512,128]{1,0:T(8,128)(2,1)S(1)}, u32[]{:S(2)}, u32[]{:S(2)}) collective-permute-start(bf16[512,128]{1,0:T(8,128)(2,1)S(1)} %broadcast_select_fusion), channel_id=1, source_target_pairs={{0,1},{1,0},{2,5},{3,4},{4,3},{5,2},{6,7},{7,6},{8,9},{9,8},{10,13... | collective-permute-start | bytes 393224 | tf_op jit(solution)/shard_map/ppermute | solution.py:366
  8.7 1.1 %copy-start.2 = (bf16[1,1,1,3072,128]{4,3,2,1,0:T(8,128)(2,1)S(1)}, bf16[1,1,1,3072,128]{4,3,2,1,0:T(8,128)(2,1)}, u32[]{:S(2)}) copy-start(bf16[1,1,1,3072,128]{4,3,2,1,0:T(8,128)(2,1)} %param.7) | copy-start | bytes 2359300
  13.0 1.3 %collective-permute-start.3 = (bf16[512,128]{1,0:T(8,128)(2,1)S(1)}, bf16[512,128]{1,0:T(8,128)(2,1)S(1)}, u32[]{:S(2)}, u32[]{:S(2)}) collective-permute-start(bf16[512,128]{1,0:T(8,128)(2,1)S(1)} %collective-permute-done), channel_id=1, source_target_pairs={{0,2},{1,3},{2,0},{3,1},{4,6},{5,7},{6,4},{7,5},{8,10},{9,11},{10,... | collective-permute-start | bytes 393224 | tf_op jit(solution)/shard_map/ppermute | solution.py:366
  13.0 1.5 %collective-permute-start.4 = (bf16[512,128]{1,0:T(8,128)(2,1)S(1)}, bf16[512,128]{1,0:T(8,128)(2,1)S(1)}, u32[]{:S(2)}, u32[]{:S(2)}) collective-permute-start(bf16[512,128]{1,0:T(8,128)(2,1)S(1)} %collective-permute-done.2), channel_id=1, source_target_pairs={{0,2},{1,3},{2,0},{3,1},{4,6},{5,7},{6,4},{7,5},{8,10},{9,11},{10,... | collective-permute-start | bytes 393224 | tf_op jit(solution)/shard_map/ppermute | solution.py:366
  19.8 4.8 %collective-permute-start.5 = (f32[4,28,16,128]{3,2,1,0:T(8,128)}, f32[4,28,16,128]{3,2,1,0:T(8,128)}, u32[]{:S(2)}, u32[]{:S(2)}) collective-permute-start(f32[4,28,16,128]{3,2,1,0:T(8,128)} %shard_map.87), channel_id=1, source_target_pairs={{0,2},{1,3},{2,0},{3,1},{4,6},{5,7},{6,4},{7,5},{8,10},{9,11},{10,... | collective-permute-start | bytes 2752520 | tf_op jit(solution)/shard_map/ppermute | solution.py:366
  24.6 2.0 %copy-start.1 = (bf16[27,128,128]{2,1,0:T(8,128)(2,1)S(1)}, bf16[27,128,128]{2,1,0:T(8,128)(2,1)}, u32[]{:S(2)}) copy-start(bf16[27,128,128]{2,1,0:T(8,128)(2,1)} %param.8) | copy-start | bytes 2654212
  26.1 10.4 %collective-permute-start.6 = (f16[2,28,16,128]{3,2,1,0:T(8,128)(2,1)S(1)}, f16[2,28,16,128]{3,2,1,0:T(8,128)(2,1)S(1)}, u32[]{:S(2)}, u32[]{:S(2)}) collective-permute-start(f16[2,28,16,128]{3,2,1,0:T(8,128)(2,1)S(1)} %get-tuple-element.42), channel_id=1, source_target_pairs={{0,4},{1,5},{2,3},{3,2},{4,0},{5,1},{6,7},{7,6},{8,12},{9,13},{10,... | collective-permute-start | bytes 688136 | tf_op jit(solution)/shard_map/ppermute | solution.py:366
  36.9 4.9 %collective-permute-start.7 = (f16[1,28,16,128]{3,2,1,0:T(8,128)(2,1)S(1)}, f16[1,28,16,128]{3,2,1,0:T(8,128)(2,1)S(1)}, u32[]{:S(2)}, u32[]{:S(2)}) collective-permute-start(f16[1,28,16,128]{3,2,1,0:T(8,128)(2,1)S(1)} %get-tuple-element.46), channel_id=1, source_target_pairs={{0,1},{1,0},{2,6},{3,7},{4,5},{5,4},{6,2},{7,3},{8,9},{9,8},{10,14... | collective-permute-start | bytes 344072 | tf_op jit(solution)/shard_map/ppermute | solution.py:366
  38.4 3.7 %collective-permute-start.8 = (f32[12,128,128]{2,1,0:T(8,128)S(1)}, f32[12,128,128]{2,1,0:T(8,128)S(1)}, u32[]{:S(2)}, u32[]{:S(2)}) collective-permute-start(f32[12,128,128]{2,1,0:T(8,128)S(1)} %get-tuple-element.47), channel_id=1, source_target_pairs={{0,2},{1,3},{2,0},{3,1},{4,6},{5,7},{6,4},{7,5},{8,10},{9,11},{10,... | collective-permute-start | bytes 2359304 | tf_op jit(solution)/shard_map/ppermute | solution.py:366
  42.0 8.7 %collective-permute-start.9 = (f16[1,28,16,128]{3,2,1,0:T(8,128)(2,1)S(1)}, f16[1,28,16,128]{3,2,1,0:T(8,128)(2,1)S(1)}, u32[]{:S(2)}, u32[]{:S(2)}) collective-permute-start(f16[1,28,16,128]{3,2,1,0:T(8,128)(2,1)S(1)} %select_convert_fusion.2), channel_id=1, source_target_pairs={{0,16},{1,17},{2,18},{3,19},{4,20},{5,21},{6,22},{7,23},{8,24},{9,... | collective-permute-start | bytes 344072 | tf_op jit(solution)/shard_map/ppermute | solution.py:366
  44.7 12.3 %collective-permute-start.12 = (f32[4,128,128]{2,1,0:T(8,128)S(1)}, f32[4,128,128]{2,1,0:T(8,128)S(1)}, u32[]{:S(2)}, u32[]{:S(2)}) collective-permute-start(f32[4,128,128]{2,1,0:T(8,128)S(1)} %get-tuple-element.69), channel_id=1, source_target_pairs={{0,1},{1,0},{2,5},{3,4},{4,3},{5,2},{6,7},{7,6},{8,9},{9,8},{10,13... | collective-permute-start | bytes 786440 | tf_op jit(solution)/shard_map/ppermute | solution.py:366
  46.3 10.7 %collective-permute-start.11 = (f32[4,128,128]{2,1,0:T(8,128)S(1)}, f32[4,128,128]{2,1,0:T(8,128)S(1)}, u32[]{:S(2)}, u32[]{:S(2)}) collective-permute-start(f32[4,128,128]{2,1,0:T(8,128)S(1)} %get-tuple-element.70), channel_id=1, source_target_pairs={{0,1},{1,0},{2,4},{3,5},{4,2},{5,3},{6,7},{7,6},{8,9},{9,8},{10,12... | collective-permute-start | bytes 786440 | tf_op jit(solution)/shard_map/ppermute | solution.py:366
  51.0 5.7 %collective-permute-start.10 = (f16[1,28,16,128]{3,2,1,0:T(8,128)(2,1)S(1)}, f16[1,28,16,128]{3,2,1,0:T(8,128)(2,1)S(1)}, u32[]{:S(2)}, u32[]{:S(2)}) collective-permute-start(f16[1,28,16,128]{3,2,1,0:T(8,128)(2,1)S(1)} %select_convert_fusion.1), channel_id=1, source_target_pairs={{0,8},{1,9},{2,10},{3,11},{4,12},{5,13},{6,14},{7,15},{8,0},{9,1},... | collective-permute-start | bytes 344072 | tf_op jit(solution)/shard_map/ppermute | solution.py:366
  57.0 5.9 %collective-permute-start.13 = (f16[1,28,16,128]{3,2,1,0:T(8,128)(2,1)S(1)}, f16[1,28,16,128]{3,2,1,0:T(8,128)(2,1)S(1)}, u32[]{:S(2)}, u32[]{:S(2)}) collective-permute-start(f16[1,28,16,128]{3,2,1,0:T(8,128)(2,1)S(1)} %select_convert_fusion), channel_id=1, source_target_pairs={{0,1},{1,0},{2,6},{3,7},{4,5},{5,4},{6,2},{7,3},{8,9},{9,8},{10,14... | collective-permute-start | bytes 344072 | tf_op jit(solution)/shard_map/ppermute | solution.py:366
  58.0 6.8 %collective-permute-start.15 = (f32[4,128,128]{2,1,0:T(8,128)S(1)}, f32[4,128,128]{2,1,0:T(8,128)S(1)}, u32[]{:S(2)}, u32[]{:S(2)}) collective-permute-start(f32[4,128,128]{2,1,0:T(8,128)S(1)} %collective-permute-done.12), channel_id=1, source_target_pairs={{0,2},{1,3},{2,0},{3,1},{4,6},{5,7},{6,4},{7,5},{8,10},{9,11},{10,... | collective-permute-start | bytes 786440 | tf_op jit(solution)/shard_map/ppermute | solution.py:366
  62.9 2.0 %copy-start.4 = (s32[1,1,1,4]{3,2,1,0:T(1,128)S(1)}, s32[1,1,1,4]{3,2,1,0:T(1,128)}, u32[]{:S(2)}) copy-start(s32[1,1,1,4]{3,2,1,0:T(1,128)} %param.10) | copy-start | bytes 52
  62.9 6.6 %collective-permute-start.16 = (f16[2,28,16,128]{3,2,1,0:T(8,128)(2,1)S(1)}, f16[2,28,16,128]{3,2,1,0:T(8,128)(2,1)S(1)}, u32[]{:S(2)}, u32[]{:S(2)}) collective-permute-start(f16[2,28,16,128]{3,2,1,0:T(8,128)(2,1)S(1)} %pad_maximum_fusion), channel_id=1, source_target_pairs={{0,2},{1,3},{2,0},{3,1},{4,6},{5,7},{6,4},{7,5},{8,10},{9,11},{10,... | collective-permute-start | bytes 688136 | tf_op jit(solution)/shard_map/ppermute | solution.py:366
  63.5 6.0 %collective-permute-start.14 = (f16[2,28,16,128]{3,2,1,0:T(8,128)(2,1)S(1)}, f16[2,28,16,128]{3,2,1,0:T(8,128)(2,1)S(1)}, u32[]{:S(2)}, u32[]{:S(2)}) collective-permute-start(f16[2,28,16,128]{3,2,1,0:T(8,128)(2,1)S(1)} %pad_maximum_fusion), channel_id=1, source_target_pairs={{0,4},{1,5},{2,3},{3,2},{4,0},{5,1},{6,7},{7,6},{8,12},{9,13},{10,... | collective-permute-start | bytes 688136 | tf_op jit(solution)/shard_map/ppermute | solution.py:366
  69.5 1.5 %collective-permute-start.17 = (f16[2,28,16,128]{3,2,1,0:T(8,128)(2,1)S(1)}, f16[2,28,16,128]{3,2,1,0:T(8,128)(2,1)S(1)}, u32[]{:S(2)}, u32[]{:S(2)}) collective-permute-start(f16[2,28,16,128]{3,2,1,0:T(8,128)(2,1)S(1)} %collective-permute-done.14), channel_id=1, source_target_pairs={{0,2},{1,3},{2,0},{3,1},{4,6},{5,7},{6,4},{7,5},{8,10},{9,11},{10,... | collective-permute-start | bytes 688136 | tf_op jit(solution)/shard_map/ppermute | solution.py:366

commit v4 on v3

--- a/solution.py
+++ b/solution.py
@@ -25,8 +25,11 @@
     return pl.CostEstimate(flops=flops, bytes_accessed=4 * 2**20, transcendentals=0)
 
 
-def outgoing_kernel(sent_ref, count_ref, x_ref, out_ref, sems):
+def outgoing_kernel(sent_hbm, count_ref, x_ref, out_ref, sent_ref, sems):
     num_sent = out_ref.shape[0]
+    copy = pltpu.make_async_copy(sent_hbm, sent_ref, sems.at[num_sent])
+    copy.start()
+    copy.wait()
     copies = [
         pltpu.make_async_copy(x_ref.at[sent_ref[s]], out_ref.at[s], sems.at[s])
         for s in range(num_sent)
@@ -44,15 +47,21 @@
 
 def outgoing(sent_ids, count, blocks):
     num_sent = sent_ids.shape[0]
+    sent_ids, blocks = (
+        pltpu.with_memory_space_constraint(a, pltpu.HBM) for a in (sent_ids, blocks)
+    )
     return pl.pallas_call(
         outgoing_kernel,
         out_shape=jax.ShapeDtypeStruct((num_sent,) + blocks.shape[1:], blocks.dtype),
-        in_specs=[SMEM, SMEM, HBM],
+        in_specs=[HBM, SMEM, HBM],
         out_specs=VMEM,
-        scratch_shapes=[pltpu.SemaphoreType.DMA((num_sent,))],
+        scratch_shapes=[
+            pltpu.SMEM(sent_ids.shape, jnp.int32),
+            pltpu.SemaphoreType.DMA((num_sent + 1,)),
+        ],
         compiler_params=params(),
         cost_estimate=pl.CostEstimate(flops=0, bytes_accessed=2**18, transcendentals=0),
-    )(sent_ids, count, pltpu.with_memory_space_constraint(blocks, pltpu.HBM))
+    )(sent_ids, count, blocks)
 
 
 def input_terms_kernel(halo_spans, picks, grad_ref, weight_ref, own_ref, *rest):
@@ -256,6 +265,8 @@
 
 def assemble_kernel(order_ref, *rest):
     *piece_refs, out_ref, sems = rest
+    if piece_refs[-1].shape == out_ref.shape:
+        piece_refs = piece_refs[:-1]
     chunks = [ref.at[r] for ref in piece_refs for r in range(ref.shape[0])]
     size = chunks[0].shape[1]
     copies = []
@@ -272,17 +283,17 @@
         copy.wait()
 
 
-def assemble(order, pieces):
+def assemble(order, pieces, shape, into=()):
     count = sum(p.shape[0] for p in pieces)
-    _, slots, size, channels = pieces[0].shape
     return pl.pallas_call(
         assemble_kernel,
-        out_shape=jax.ShapeDtypeStruct((slots - 1, count * size, channels), F32),
-        in_specs=[SMEM] + [ANY] * len(pieces),
+        out_shape=jax.ShapeDtypeStruct(shape, F32),
+        in_specs=[SMEM] + [ANY] * (len(pieces) + len(into)),
         out_specs=ANY,
         scratch_shapes=[pltpu.SemaphoreType.DMA((count,))],
-        compiler_params=params(),
-    )(order, *pieces)
+        input_output_aliases={1 + len(pieces): 0} if into else {},
+        compiler_params=params(),
+    )(order, *pieces, *into)
 
 
 def local(features, cotangent, weights, tables, send_lists, counts):
@@ -380,7 +391,7 @@
         beside = exchange(sent, cores)
         first = exchange(sent, straight)
         second = exchange(jnp.where(middle, sent, beside), across)
-        first, second, turned_own = lax.optimization_barrier((first, second, turned_own))
+        second, turned_own = lax.optimization_barrier((second, turned_own))
         passed = [exchange(first, cores), exchange(second, cores)]
         extended = [blocks] + [to_blocks(a) for a in [beside, first, second] + passed]
 
@@ -398,7 +409,6 @@
 
         near_order = jnp.concatenate([core * 4 + chunk, places(core)])
         far_order = jnp.concatenate([(1 - core) * 4 + chunk, places(1 - core)])
-        order = jnp.concatenate([keep, send])
         blocks_turned = [turned_own] + extended[1:]
         far = weight_terms(far_order, picks, kept_grads, blocks_turned, offsets, scale, 4)
         kept_grads, far = lax.optimization_barrier((kept_grads, far))
@@ -429,7 +439,7 @@
             unit = jnp.exp2(wide[:, offsets:])
             return jnp.where(slot_id < offsets, wide * unit, unit * 32768.0)
 
-        near = near + exchange(far, cores)
+        near = near + decode(exchange(encode(far), cores))
         message, pair = encode(near[2:]), near[:2]
         message, pair, late_grads = lax.optimization_barrier((message, pair, kept_grads))
         spans = [(r * num_sent, num_sent) for r in range(5)]
@@ -438,24 +448,25 @@
         )
         back = exchange(inner_terms, cores)
         pair = pair + decode(exchange(message, x_or_y))
-        message, part, own_terms = lax.optimization_barrier(
-            (encode(pair[1:]), pair[:1], own_terms)
-        )
+        message, part, own_terms, late_picks = lax.optimization_barrier(
+            (encode(pair[1:]), pair[:1], own_terms, picks)
+        )
+        cuts = [num_blocks * third // 24 * 8 for third in range(3)] + [num_blocks]
+        output = output_blocks(late_picks, weights, extended, (cuts[0], cuts[1]))
         message = encode(part + decode(exchange(message, y_or_x)))
-        message, back, late_picks = lax.optimization_barrier((message, back, picks))
+        message, back, late_picks, output = lax.optimization_barrier(
+            (message, back, late_picks, output)
+        )
         first_back = exchange(first_terms + back[num_sent : 2 * num_sent], straight)
         second_back = exchange(second_terms + back[2 * num_sent :], across)
-        middle_block = num_blocks // 2
-        upper = output_blocks(late_picks, weights, extended, (0, middle_block))
+        output = output_blocks(late_picks, weights, extended, (cuts[1], cuts[2]), (output,))
         part = decode(message) + decode(exchange(message, z_far))
-        message, upper = lax.optimization_barrier((encode(part), upper))
+        message, output = lax.optimization_barrier((encode(part), output))
         part = decode(message) + decode(exchange(message, z_near))
         message, first_back, second_back, late_picks = lax.optimization_barrier(
             (encode(part), first_back, second_back, late_picks)
         )
-        output = output_blocks(
-            late_picks, weights, extended, (middle_block, num_blocks), (upper,)
-        )
+        output = output_blocks(late_picks, weights, extended, (cuts[2], cuts[3]), (output,))
         passed_back = exchange(second_back, cores)
         returned = [
             back[:num_sent] + jnp.where(middle, second_back + passed_back, 0.0),
@@ -464,10 +475,14 @@
         pair = jnp.concatenate([message, exchange(message, y_or_x)])
         pair, output, own_terms = lax.optimization_barrier((pair, output, own_terms))
         input_grad = input_grad_blocks(sent_ids, count, own_terms, returned)
+        early_order = jnp.concatenate([keep[:2], send[:2]])
+        late_order = jnp.concatenate([keep[2:], send[2:]])
+        early = [decode(m) for m in (pair, exchange(pair, cores))]
+        weight_grad = assemble(early_order, early, weights.shape)
         rest = exchange(pair, x_or_y)
-        rest, input_grad = lax.optimization_barrier((rest, input_grad))
-        messages = [pair, rest, exchange(pair, cores), exchange(rest, cores)]
-        weight_grad = assemble(order, [decode(m) for m in messages])
+        rest, input_grad, weight_grad = lax.optimization_barrier((rest, input_grad, weight_grad))
+        late = [decode(m) for m in (rest, exchange(rest, cores))]
+        weight_grad = assemble(late_order, late, weights.shape, [weight_grad])
 
     else:
         beside = [lax.ppermute(sent, "sy", route) for route in along_y]

time: 73.5 us -> 71.5 us (0.973)
  starting transfers between devices: 16.3 us -> 13.4 us
  Pallas kernels: 33.4 us -> 34.3 us
    ppermute x18, starting transfers between devices: 16.3 us -> 13.4 us  [exchange(): return lax.ppermute(array, AXES, route)]
    add x1, other arithmetic: 1.37 us -> 0.17 us  [local(): near = near + decode(exchange(encode(far), cores))]
    pallas_call x1 -> x2, Pallas kernels: 1.81 us -> 2.97 us  [assemble(): pl.pallas_call(assemble_kernel, out_shape=jax.ShapeDtypeStruct(shape, F32...]
    convert_element_type x3 -> x4, other arithmetic: 0.31 us -> 1.25 us  [encode(): return jnp.where(slot_id < offsets, values, exponent).astype(jnp.float16)]
    pallas_call x2, Pallas kernels: 9.62 us -> 8.7 us  [weight_terms(): pl.pallas_call(functools.partial(weight_terms_kernel, scale, group), out_...]
    pallas_call x2 -> x3, Pallas kernels: 8.75 us -> 9.28 us  [output_blocks(): pl.pallas_call(functools.partial(output_kernel, group, span, len(done)),...]
    unnamed x10 -> x8, local copies, waits for them, and re-layouts: 1.79 us -> 1.88 us
  transfers between devices with their start and end apart: 18 -> 18, of which waited for: 7 -> 9; matrix products, arithmetic and copies ran while one was open for 3% -> 4% of each run, Pallas kernels for 34% -> 38%
where the time goes in v4:
time: 71.5 us; the launch traced here: 71.2 us
  Pallas kernels  34.3 us (48%)
  waiting for transfers between devices  15.5 us (22%)
  starting transfers between devices  13.4 us (19%)
  other arithmetic  4.2 us (6%)
  local copies, waits for them, and re-layouts  2.02 us (3%)
  between operations  1.79 us (3%)
    ppermute x18, waiting for transfers between devices, exchange(): return lax.ppermute(array, AXES, route)  15.5 us
    ppermute x18, starting transfers between devices, exchange(): return lax.ppermute(array, AXES, route)  13.4 us
    pallas_call x1, Pallas kernels, input_terms(): pl.pallas_call(functools.partial(input_terms_kernel, halo_spans), out_sha...  10 us
    pallas_call x3, Pallas kernels, output_blocks(): pl.pallas_call(functools.partial(output_kernel, group, span, len(done)),...  9.28 us
    pallas_call x2, Pallas kernels, weight_terms(): pl.pallas_call(functools.partial(weight_terms_kernel, scale, group), out_...  8.7 us
    pallas_call x2, Pallas kernels, assemble(): pl.pallas_call(assemble_kernel, out_shape=jax.ShapeDtypeStruct(shape, F32...  2.97 us
    unnamed x8, local copies, waits for them, and re-layouts  1.88 us
    pallas_call x1, Pallas kernels, input_grad_blocks(): pl.pallas_call(input_grad_kernel, out_shape=jax.ShapeDtypeStruct(own.shap...  1.55 us
  transfers between devices with their start and end apart: 18, of which 9 were waited for; matrix products, arithmetic and copies ran while one was open for 4% of the time, Pallas kernels for 38%

profile of v4, /device:TPU:0, one launch (start us, length us, event | category | flops | bytes accessed | tf_op | source)
XLA Modules:
  0.0 71.2 jit_solution(7309526200508317398)
XLA Ops:
  1.4 1.5 %shard_map.86 = bf16[4,128,128]{2,1,0:T(8,128)(2,1)S(1)} custom-call(s32[4]{0:T(128)} %bitcast.146, s32[1]{0:T(128)} %bitcast.105.count_ref, bf16[24,128,128]{2,1,0:T(8,128)(2,1)} %bitcast.107), custom_call_target="tpu_custom_call" | custom-call | bytes 262144 | tf_op jit(solution)/shard_map/pallas_call | solution.py:53
  2.9 3.0 %collective-permute-start.2 = (bf16[512,128]{1,0:T(8,128)(2,1)S(1)}, bf16[512,128]{1,0:T(8,128)(2,1)S(1)}, u32[]{:S(2)}, u32[]{:S(2)}) collective-permute-start(bf16[512,128]{1,0:T(8,128)(2,1)S(1)} %bitcast.144), channel_id=1, source_target_pairs={{0,1},{1,0},{2,4},{3,5},{4,2},{5,3},{6,7},{7,6},{8,9},{9,8},{10,12... | collective-permute-start | bytes 393224 | tf_op jit(solution)/shard_map/ppermute | solution.py:377
  7.3 1.3 %collective-permute-start.1 = (bf16[512,128]{1,0:T(8,128)(2,1)S(1)}, bf16[512,128]{1,0:T(8,128)(2,1)S(1)}, u32[]{:S(2)}, u32[]{:S(2)}) collective-permute-start(bf16[512,128]{1,0:T(8,128)(2,1)S(1)} %broadcast_select_fusion), channel_id=1, source_target_pairs={{0,1},{1,0},{2,5},{3,4},{4,3},{5,2},{6,7},{7,6},{8,9},{9,8},{10,13... | collective-permute-start | bytes 393224 | tf_op jit(solution)/shard_map/ppermute | solution.py:377
  8.6 1.1 %copy-done.2 = bf16[1,1,1,3072,128]{4,3,2,1,0:T(8,128)(2,1)S(1)} copy-done((bf16[1,1,1,3072,128]{4,3,2,1,0:T(8,128)(2,1)S(1)}, bf16[1,1,1,3072,128]{4,3,2,1,0:T(8,128)(2,1)}, u32[]{:S(2)}) %copy-start.2) | copy-done | bytes 786456
  10.1 3.6 %collective-permute-done.1 = bf16[512,128]{1,0:T(8,128)(2,1)S(1)} collective-permute-done((bf16[512,128]{1,0:T(8,128)(2,1)S(1)}, bf16[512,128]{1,0:T(8,128)(2,1)S(1)}, u32[]{:S(2)}, u32[]{:S(2)}) %collective-permute-start.1) | collective-permute-done | bytes 131104 | tf_op jit(solution)/shard_map/ppermute | solution.py:377
  13.8 1.3 %collective-permute-done.4 = bf16[512,128]{1,0:T(8,128)(2,1)S(1)} collective-permute-done((bf16[512,128]{1,0:T(8,128)(2,1)S(1)}, bf16[512,128]{1,0:T(8,128)(2,1)S(1)}, u32[]{:S(2)}, u32[]{:S(2)}) %collective-permute-start.4) | collective-permute-done | bytes 131104 | tf_op jit(solution)/shard_map/ppermute | solution.py:377
  15.1 4.3 %shard_map.87 = f32[4,28,16,128]{3,2,1,0:T(8,128)S(1)} custom-call(s32[8]{0:T(128)S(1)} %pad_add_fusion.1.order_ref, s32[24,27]{1,0:T(8,128)S(1)} %fusion.21.picks, bf16[3072,128]{1,0:T(8,128)(2,1)S(1)} %bitcast.116, bf16[24,128,128]{2,1,0:T(8,128)(2,1)S(1)} %get-tuple-element.38.rest_0_, bf16[4,128,128]{2,1,0:T(8,128)(2,1)S(1)} %bitcast.118, ...), custom_call_target="tpu_custom_call" | custom-call | flops 10000000 | bytes 4194304 | tf_op jit(solution)/shard_map/pallas_call | solution.py:179
  20.6 4.3 %shard_map.88 = f32[4,28,16,128]{3,2,1,0:T(8,128)S(1)} custom-call(s32[8]{0:T(128)S(1)} %pad_add_fusion.order_ref, s32[24,27]{1,0:T(8,128)S(1)} %fusion.21.picks, bf16[3072,128]{1,0:T(8,128)(2,1)S(1)} %bitcast.117, bf16[24,128,128]{2,1,0:T(8,128)(2,1)S(1)} %get-tuple-element.38.rest_0_, bf16[4,128,128]{2,1,0:T(8,128)(2,1)S(1)} %bitcast.119, ...), custom_call_target="tpu_custom_call" | custom-call | flops 10000000 | bytes 4194304 | tf_op jit(solution)/shard_map/pallas_call | solution.py:179
  26.3 10.0 %shard_map.89 = (f32[24,128,128]{2,1,0:T(8,128)S(1)}, f32[12,128,128]{2,1,0:T(8,128)S(1)}, f32[4,128,128]{2,1,0:T(8,128)S(1)}, f32[4,128,128]{2,1,0:T(8,128)S(1)}) custom-call(s32[24,27]{1,0:T(8,128)S(1)} %fusion.21.picks, bf16[24,128,128]{2,1,0:T(8,128)(2,1)S(1)} %get-tuple-element.44.grad_ref, bf16[3456,128]{1,0:T(8,128)(2,1)S(1)} %bitcast.112), custom_call_target="tpu_custom_call" | custom-call | flops 10000000 | bytes 4194304 | tf_op jit(solution)/shard_map/pallas_call | solution.py:103
  36.6 1.3 %collective-permute-start.7 = (f16[1,28,16,128]{3,2,1,0:T(8,128)(2,1)S(1)}, f16[1,28,16,128]{3,2,1,0:T(8,128)(2,1)S(1)}, u32[]{:S(2)}, u32[]{:S(2)}) collective-permute-start(f16[1,28,16,128]{3,2,1,0:T(8,128)(2,1)S(1)} %get-tuple-element.47), channel_id=1, source_target_pairs={{0,1},{1,0},{2,6},{3,7},{4,5},{5,4},{6,2},{7,3},{8,9},{9,8},{10,14... | collective-permute-start | bytes 344072 | tf_op jit(solution)/shard_map/ppermute | solution.py:377
  38.0 2.8 %shard_map.90.rest_0_ = bf16[1024,128]{1,0:T(8,128)(2,1)S(1)} custom-call(s32[24,27]{1,0:T(8,128)S(1)} %fusion.21.picks, bf16[3456,128]{1,0:T(8,128)(2,1)S(1)} %bitcast.113, bf16[24,128,128]{2,1,0:T(8,128)(2,1)S(1)} %bitcast.109, bf16[4,128,128]{2,1,0:T(8,128)(2,1)S(1)} %bitcast.120, bf16[4,128,128]{2,1,0:T(8,128)(2,1)S(1)} %bitcast.125, ...), custom_call_target="tpu_custom_call" | custom-call | flops 10000000 | bytes 4194304 | tf_op jit(solution)/shard_map/pallas_call | solution.py:229
  41.8 2.7 %collective-permute-start.9 = (f16[1,28,16,128]{3,2,1,0:T(8,128)(2,1)S(1)}, f16[1,28,16,128]{3,2,1,0:T(8,128)(2,1)S(1)}, u32[]{:S(2)}, u32[]{:S(2)}) collective-permute-start(f16[1,28,16,128]{3,2,1,0:T(8,128)(2,1)S(1)} %select_convert_fusion.3), channel_id=1, source_target_pairs={{0,16},{1,17},{2,18},{3,19},{4,20},{5,21},{6,22},{7,23},{8,24},{9,... | collective-permute-start | bytes 344072 | tf_op jit(solution)/shard_map/ppermute | solution.py:377
  44.5 1.3 %collective-permute-start.12 = (f32[4,128,128]{2,1,0:T(8,128)S(1)}, f32[4,128,128]{2,1,0:T(8,128)S(1)}, u32[]{:S(2)}, u32[]{:S(2)}) collective-permute-start(f32[4,128,128]{2,1,0:T(8,128)S(1)} %get-tuple-element.77), channel_id=1, source_target_pairs={{0,1},{1,0},{2,5},{3,4},{4,3},{5,2},{6,7},{7,6},{8,9},{9,8},{10,13... | collective-permute-start | bytes 786440 | tf_op jit(solution)/shard_map/ppermute | solution.py:377
  46.6 2.8 %shard_map.91.rest_0_ = bf16[2048,128]{1,0:T(8,128)(2,1)S(1)} custom-call(s32[24,27]{1,0:T(8,128)S(1)} %fusion.21.picks, bf16[3456,128]{1,0:T(8,128)(2,1)S(1)} %bitcast.114, bf16[1024,128]{1,0:T(8,128)(2,1)S(1)} %shard_map.90.rest_0_, bf16[24,128,128]{2,1,0:T(8,128)(2,1)S(1)} %bitcast.110, bf16[4,128,128]{2,1,0:T(8,128)(2,1)S(1)} %bitcast.121, ...), custom_call_target="tpu_custom_call" | custom-call | flops 10000000 | bytes 4194304 | tf_op jit(solution)/shard_map/pallas_call | solution.py:229
  50.4 1.0 %collective-permute-start.10 = (f16[1,28,16,128]{3,2,1,0:T(8,128)(2,1)S(1)}, f16[1,28,16,128]{3,2,1,0:T(8,128)(2,1)S(1)}, u32[]{:S(2)}, u32[]{:S(2)}) collective-permute-start(f16[1,28,16,128]{3,2,1,0:T(8,128)(2,1)S(1)} %select_convert_fusion.2), channel_id=1, source_target_pairs={{0,8},{1,9},{2,10},{3,11},{4,12},{5,13},{6,14},{7,15},{8,0},{9,1},... | collective-permute-start | bytes 344072 | tf_op jit(solution)/shard_map/ppermute | solution.py:377
  51.4 3.8 %collective-permute-done.10 = f16[1,28,16,128]{3,2,1,0:T(8,128)(2,1)S(1)} collective-permute-done((f16[1,28,16,128]{3,2,1,0:T(8,128)(2,1)S(1)}, f16[1,28,16,128]{3,2,1,0:T(8,128)(2,1)S(1)}, u32[]{:S(2)}, u32[]{:S(2)}) %collective-permute-start.10) | collective-permute-done | bytes 114720 | tf_op jit(solution)/shard_map/ppermute | solution.py:377
  55.5 1.1 %collective-permute-done.11.rest_1_ = f32[4,128,128]{2,1,0:T(8,128)S(1)} collective-permute-done((f32[4,128,128]{2,1,0:T(8,128)S(1)}, f32[4,128,128]{2,1,0:T(8,128)S(1)}, u32[]{:S(2)}, u32[]{:S(2)}) %collective-permute-start.11) | collective-permute-done | bytes 262176 | tf_op jit(solution)/shard_map/ppermute | solution.py:377
  56.6 1.0 %collective-permute-start.13 = (f16[1,28,16,128]{3,2,1,0:T(8,128)(2,1)S(1)}, f16[1,28,16,128]{3,2,1,0:T(8,128)(2,1)S(1)}, u32[]{:S(2)}, u32[]{:S(2)}) collective-permute-start(f16[1,28,16,128]{3,2,1,0:T(8,128)(2,1)S(1)} %select_convert_fusion.1), channel_id=1, source_target_pairs={{0,1},{1,0},{2,6},{3,7},{4,5},{5,4},{6,2},{7,3},{8,9},{9,8},{10,14... | collective-permute-start | bytes 344072 | tf_op jit(solution)/shard_map/ppermute | solution.py:377
  57.7 3.7 %shard_map.92 = bf16[3072,128]{1,0:T(8,128)(2,1)} custom-call(s32[24,27]{1,0:T(8,128)S(1)} %fusion.21.picks, bf16[3456,128]{1,0:T(8,128)(2,1)S(1)} %bitcast.115, bf16[2048,128]{1,0:T(8,128)(2,1)S(1)} %shard_map.91.rest_0_, bf16[24,128,128]{2,1,0:T(8,128)(2,1)S(1)} %bitcast.111, bf16[4,128,128]{2,1,0:T(8,128)(2,1)S(1)} %bitcast.122, ...), custom_call_target="tpu_custom_call" | custom-call | flops 10000000 | bytes 4194304 | tf_op jit(solution)/shard_map/pallas_call | solution.py:229
  62.2 1.6 %shard_map.93 = bf16[24,128,128]{2,1,0:T(8,128)(2,1)} custom-call(s32[4]{0:T(128)S(1)} %bitcast.147, s32[1]{0:T(128)} %bitcast.106.count_ref, f32[24,128,128]{2,1,0:T(8,128)S(1)} %get-tuple-element.63.own_ref, f32[4,128,128]{2,1,0:T(8,128)S(1)} %select_add_fusion.2.rest_0_, f32[4,128,128]{2,1,0:T(8,128)S(1)} %collective-permute-done.11.rest_1_), custom_call_target="tpu_custom_call" | custom-call | flops 10000000 | bytes 4194304 | tf_op jit(solution)/shard_map/pallas_call | solution.py:256
  64.0 1.5 %shard_map.94.rest_2_ = f32[27,128,128]{2,1,0:T(8,128)} custom-call(s32[4]{0:T(128)S(1)} %pad_add_fusion.2.order_ref, f32[2,28,16,128]{3,2,1,0:T(8,128)S(1)} %get-tuple-element.116.rest_0_, f32[2,28,16,128]{3,2,1,0:T(8,128)S(1)} %get-tuple-element.115.rest_1_), custom_call_target="tpu_custom_call" | custom-call | tf_op jit(solution)/shard_map/pallas_call | solution.py:288
  65.5 2.6 %collective-permute-done.14 = f16[2,28,16,128]{3,2,1,0:T(8,128)(2,1)S(1)} collective-permute-done((f16[2,28,16,128]{3,2,1,0:T(8,128)(2,1)S(1)}, f16[2,28,16,128]{3,2,1,0:T(8,128)(2,1)S(1)}, u32[]{:S(2)}, u32[]{:S(2)}) %collective-permute-start.14) | collective-permute-done | bytes 229408 | tf_op jit(solution)/shard_map/ppermute | solution.py:377
  68.2 1.4 %collective-permute-done.17 = f16[2,28,16,128]{3,2,1,0:T(8,128)(2,1)S(1)} collective-permute-done((f16[2,28,16,128]{3,2,1,0:T(8,128)(2,1)S(1)}, f16[2,28,16,128]{3,2,1,0:T(8,128)(2,1)S(1)}, u32[]{:S(2)}, u32[]{:S(2)}) %collective-permute-start.17) | collective-permute-done | bytes 229408 | tf_op jit(solution)/shard_map/ppermute | solution.py:377
  69.7 1.5 %shard_map.95 = f32[27,128,128]{2,1,0:T(8,128)} custom-call(s32[4]{0:T(128)S(1)} %pad_add_fusion.3.order_ref, f32[2,28,16,128]{3,2,1,0:T(8,128)S(1)} %get-tuple-element.110.rest_0_, f32[2,28,16,128]{3,2,1,0:T(8,128)S(1)} %get-tuple-element.109.rest_1_, f32[27,128,128]{2,1,0:T(8,128)} %shard_map.94.rest_2_), custom_call_target="tpu_custom_call", output_to_operand_aliasing={{}: (3, {})} | custom-call | tf_op jit(solution)/shard_map/pallas_call | solution.py:288
  (89 shorter events, 9.0 us)
Async XLA Ops:
  0.6 8.0 %copy-start = (bf16[1,1,1,3072,128]{4,3,2,1,0:T(8,128)(2,1)S(1)}, bf16[1,1,1,3072,128]{4,3,2,1,0:T(8,128)(2,1)}, u32[]{:S(2)}) copy-start(bf16[1,1,1,3072,128]{4,3,2,1,0:T(8,128)(2,1)} %param.6) | copy-start | bytes 2359300
  2.9 7.2 %collective-permute-start.2 = (bf16[512,128]{1,0:T(8,128)(2,1)S(1)}, bf16[512,128]{1,0:T(8,128)(2,1)S(1)}, u32[]{:S(2)}, u32[]{:S(2)}) collective-permute-start(bf16[512,128]{1,0:T(8,128)(2,1)S(1)} %bitcast.144), channel_id=1, source_target_pairs={{0,1},{1,0},{2,4},{3,5},{4,2},{5,3},{6,7},{7,6},{8,9},{9,8},{10,12... | collective-permute-start | bytes 393224 | tf_op jit(solution)/shard_map/ppermute | solution.py:377
  5.9 1.3 %collective-permute-start = (bf16[512,128]{1,0:T(8,128)(2,1)S(1)}, bf16[512,128]{1,0:T(8,128)(2,1)S(1)}, u32[]{:S(2)}, u32[]{:S(2)}) collective-permute-start(bf16[512,128]{1,0:T(8,128)(2,1)S(1)} %bitcast.145), channel_id=1, source_target_pairs={{0,2},{1,3},{2,0},{3,1},{4,6},{5,7},{6,4},{7,5},{8,10},{9,11},{10,... | collective-permute-start | bytes 393224 | tf_op jit(solution)/shard_map/ppermute | solution.py:377
  7.3 6.4 %collective-permute-start.1 = (bf16[512,128]{1,0:T(8,128)(2,1)S(1)}, bf16[512,128]{1,0:T(8,128)(2,1)S(1)}, u32[]{:S(2)}, u32[]{:S(2)}) collective-permute-start(bf16[512,128]{1,0:T(8,128)(2,1)S(1)} %broadcast_select_fusion), channel_id=1, source_target_pairs={{0,1},{1,0},{2,5},{3,4},{4,3},{5,2},{6,7},{7,6},{8,9},{9,8},{10,13... | collective-permute-start | bytes 393224 | tf_op jit(solution)/shard_map/ppermute | solution.py:377
  8.6 1.1 %copy-start.2 = (bf16[1,1,1,3072,128]{4,3,2,1,0:T(8,128)(2,1)S(1)}, bf16[1,1,1,3072,128]{4,3,2,1,0:T(8,128)(2,1)}, u32[]{:S(2)}) copy-start(bf16[1,1,1,3072,128]{4,3,2,1,0:T(8,128)(2,1)} %param.7) | copy-start | bytes 2359300
  10.1 3.8 %collective-permute-start.3 = (bf16[512,128]{1,0:T(8,128)(2,1)S(1)}, bf16[512,128]{1,0:T(8,128)(2,1)S(1)}, u32[]{:S(2)}, u32[]{:S(2)}) collective-permute-start(bf16[512,128]{1,0:T(8,128)(2,1)S(1)} %collective-permute-done.2), channel_id=1, source_target_pairs={{0,2},{1,3},{2,0},{3,1},{4,6},{5,7},{6,4},{7,5},{8,10},{9,11},{10,... | collective-permute-start | bytes 393224 | tf_op jit(solution)/shard_map/ppermute | solution.py:377
  13.7 1.3 %collective-permute-start.4 = (bf16[512,128]{1,0:T(8,128)(2,1)S(1)}, bf16[512,128]{1,0:T(8,128)(2,1)S(1)}, u32[]{:S(2)}, u32[]{:S(2)}) collective-permute-start(bf16[512,128]{1,0:T(8,128)(2,1)S(1)} %collective-permute-done.1), channel_id=1, source_target_pairs={{0,2},{1,3},{2,0},{3,1},{4,6},{5,7},{6,4},{7,5},{8,10},{9,11},{10,... | collective-permute-start | bytes 393224 | tf_op jit(solution)/shard_map/ppermute | solution.py:377
  20.4 4.6 %collective-permute-start.5 = (f16[4,28,16,128]{3,2,1,0:T(8,128)(2,1)}, f16[4,28,16,128]{3,2,1,0:T(8,128)(2,1)S(1)}, u32[]{:S(2)}, u32[]{:S(2)}) collective-permute-start(f16[4,28,16,128]{3,2,1,0:T(8,128)(2,1)} %select_convert_fusion), channel_id=1, source_target_pairs={{0,2},{1,3},{2,0},{3,1},{4,6},{5,7},{6,4},{7,5},{8,10},{9,11},{10,... | collective-permute-start | bytes 1376264 | tf_op jit(solution)/shard_map/ppermute | solution.py:377
  25.1 1.2 %copy-start.1 = (bf16[27,128,128]{2,1,0:T(8,128)(2,1)S(1)}, bf16[27,128,128]{2,1,0:T(8,128)(2,1)}, u32[]{:S(2)}) copy-start(bf16[27,128,128]{2,1,0:T(8,128)(2,1)} %param.8) | copy-start | bytes 2654212
  25.5 10.8 %collective-permute-start.6 = (f16[2,28,16,128]{3,2,1,0:T(8,128)(2,1)S(1)}, f16[2,28,16,128]{3,2,1,0:T(8,128)(2,1)S(1)}, u32[]{:S(2)}, u32[]{:S(2)}) collective-permute-start(f16[2,28,16,128]{3,2,1,0:T(8,128)(2,1)S(1)} %get-tuple-element.43), channel_id=1, source_target_pairs={{0,4},{1,5},{2,3},{3,2},{4,0},{5,1},{6,7},{7,6},{8,12},{9,13},{10,... | collective-permute-start | bytes 688136 | tf_op jit(solution)/shard_map/ppermute | solution.py:377
  36.6 4.9 %collective-permute-start.7 = (f16[1,28,16,128]{3,2,1,0:T(8,128)(2,1)S(1)}, f16[1,28,16,128]{3,2,1,0:T(8,128)(2,1)S(1)}, u32[]{:S(2)}, u32[]{:S(2)}) collective-permute-start(f16[1,28,16,128]{3,2,1,0:T(8,128)(2,1)S(1)} %get-tuple-element.47), channel_id=1, source_target_pairs={{0,1},{1,0},{2,6},{3,7},{4,5},{5,4},{6,2},{7,3},{8,9},{9,8},{10,14... | collective-permute-start | bytes 344072 | tf_op jit(solution)/shard_map/ppermute | solution.py:377
  38.0 3.8 %collective-permute-start.8 = (f32[12,128,128]{2,1,0:T(8,128)S(1)}, f32[12,128,128]{2,1,0:T(8,128)S(1)}, u32[]{:S(2)}, u32[]{:S(2)}) collective-permute-start(f32[12,128,128]{2,1,0:T(8,128)S(1)} %get-tuple-element.48), channel_id=1, source_target_pairs={{0,2},{1,3},{2,0},{3,1},{4,6},{5,7},{6,4},{7,5},{8,10},{9,11},{10,... | collective-permute-start | bytes 2359304 | tf_op jit(solution)/shard_map/ppermute | solution.py:377
  41.8 8.3 %collective-permute-start.9 = (f16[1,28,16,128]{3,2,1,0:T(8,128)(2,1)S(1)}, f16[1,28,16,128]{3,2,1,0:T(8,128)(2,1)S(1)}, u32[]{:S(2)}, u32[]{:S(2)}) collective-permute-start(f16[1,28,16,128]{3,2,1,0:T(8,128)(2,1)S(1)} %select_convert_fusion.3), channel_id=1, source_target_pairs={{0,16},{1,17},{2,18},{3,19},{4,20},{5,21},{6,22},{7,23},{8,24},{9,... | collective-permute-start | bytes 344072 | tf_op jit(solution)/shard_map/ppermute | solution.py:377
  44.5 11.0 %collective-permute-start.12 = (f32[4,128,128]{2,1,0:T(8,128)S(1)}, f32[4,128,128]{2,1,0:T(8,128)S(1)}, u32[]{:S(2)}, u32[]{:S(2)}) collective-permute-start(f32[4,128,128]{2,1,0:T(8,128)S(1)} %get-tuple-element.77), channel_id=1, source_target_pairs={{0,1},{1,0},{2,5},{3,4},{4,3},{5,2},{6,7},{7,6},{8,9},{9,8},{10,13... | collective-permute-start | bytes 786440 | tf_op jit(solution)/shard_map/ppermute | solution.py:377
  45.8 10.7 %collective-permute-start.11 = (f32[4,128,128]{2,1,0:T(8,128)S(1)}, f32[4,128,128]{2,1,0:T(8,128)S(1)}, u32[]{:S(2)}, u32[]{:S(2)}) collective-permute-start(f32[4,128,128]{2,1,0:T(8,128)S(1)} %get-tuple-element.78), channel_id=1, source_target_pairs={{0,1},{1,0},{2,4},{3,5},{4,2},{5,3},{6,7},{7,6},{8,9},{9,8},{10,12... | collective-permute-start | bytes 786440 | tf_op jit(solution)/shard_map/ppermute | solution.py:377
  50.4 4.9 %collective-permute-start.10 = (f16[1,28,16,128]{3,2,1,0:T(8,128)(2,1)S(1)}, f16[1,28,16,128]{3,2,1,0:T(8,128)(2,1)S(1)}, u32[]{:S(2)}, u32[]{:S(2)}) collective-permute-start(f16[1,28,16,128]{3,2,1,0:T(8,128)(2,1)S(1)} %select_convert_fusion.2), channel_id=1, source_target_pairs={{0,8},{1,9},{2,10},{3,11},{4,12},{5,13},{6,14},{7,15},{8,0},{9,1},... | collective-permute-start | bytes 344072 | tf_op jit(solution)/shard_map/ppermute | solution.py:377
  56.6 4.8 %collective-permute-start.13 = (f16[1,28,16,128]{3,2,1,0:T(8,128)(2,1)S(1)}, f16[1,28,16,128]{3,2,1,0:T(8,128)(2,1)S(1)}, u32[]{:S(2)}, u32[]{:S(2)}) collective-permute-start(f16[1,28,16,128]{3,2,1,0:T(8,128)(2,1)S(1)} %select_convert_fusion.1), channel_id=1, source_target_pairs={{0,1},{1,0},{2,6},{3,7},{4,5},{5,4},{6,2},{7,3},{8,9},{9,8},{10,14... | collective-permute-start | bytes 344072 | tf_op jit(solution)/shard_map/ppermute | solution.py:377
  57.7 4.5 %collective-permute-start.15 = (f32[4,128,128]{2,1,0:T(8,128)S(1)}, f32[4,128,128]{2,1,0:T(8,128)S(1)}, u32[]{:S(2)}, u32[]{:S(2)}) collective-permute-start(f32[4,128,128]{2,1,0:T(8,128)S(1)} %collective-permute-done.12), channel_id=1, source_target_pairs={{0,2},{1,3},{2,0},{3,1},{4,6},{5,7},{6,4},{7,5},{8,10},{9,11},{10,... | collective-permute-start | bytes 786440 | tf_op jit(solution)/shard_map/ppermute | solution.py:377
  61.4 0.9 %copy-start.3 = (s32[1,1,1,4]{3,2,1,0:T(1,128)S(1)}, s32[1,1,1,4]{3,2,1,0:T(1,128)}, u32[]{:S(2)}) copy-start(s32[1,1,1,4]{3,2,1,0:T(1,128)} %param.10) | copy-start | bytes 52
  61.4 2.4 %collective-permute-start.16 = (f16[2,28,16,128]{3,2,1,0:T(8,128)(2,1)S(1)}, f16[2,28,16,128]{3,2,1,0:T(8,128)(2,1)S(1)}, u32[]{:S(2)}, u32[]{:S(2)}) collective-permute-start(f16[2,28,16,128]{3,2,1,0:T(8,128)(2,1)S(1)} %pad_maximum_fusion), channel_id=1, source_target_pairs={{0,2},{1,3},{2,0},{3,1},{4,6},{5,7},{6,4},{7,5},{8,10},{9,11},{10,... | collective-permute-start | bytes 688136 | tf_op jit(solution)/shard_map/ppermute | solution.py:377
  62.0 6.0 %collective-permute-start.14 = (f16[2,28,16,128]{3,2,1,0:T(8,128)(2,1)S(1)}, f16[2,28,16,128]{3,2,1,0:T(8,128)(2,1)S(1)}, u32[]{:S(2)}, u32[]{:S(2)}) collective-permute-start(f16[2,28,16,128]{3,2,1,0:T(8,128)(2,1)S(1)} %pad_maximum_fusion), channel_id=1, source_target_pairs={{0,4},{1,5},{2,3},{3,2},{4,0},{5,1},{6,7},{7,6},{8,12},{9,13},{10,... | collective-permute-start | bytes 688136 | tf_op jit(solution)/shard_map/ppermute | solution.py:377
  68.0 1.5 %collective-permute-start.17 = (f16[2,28,16,128]{3,2,1,0:T(8,128)(2,1)S(1)}, f16[2,28,16,128]{3,2,1,0:T(8,128)(2,1)S(1)}, u32[]{:S(2)}, u32[]{:S(2)}) collective-permute-start(f16[2,28,16,128]{3,2,1,0:T(8,128)(2,1)S(1)} %collective-permute-done.14), channel_id=1, source_target_pairs={{0,2},{1,3},{2,0},{3,1},{4,6},{5,7},{6,4},{7,5},{8,10},{9,11},{10,... | collective-permute-start | bytes 688136 | tf_op jit(solution)/shard_map/ppermute | solution.py:377
